TPU v7x, 512 devices: a whole 4x4x16 slice. The times are simulated.
512 devices in a mesh: tm: 32 (over x_lo, z), space: 8 (over y, core), head: 2 (over x_hi).
Axes of the slice: x: 4 (x_hi: 2, x_lo: 2; x = x_hi * 2 + x_lo), y: 4, z: 16, core: 2. Of those that a mesh axis runs over, the one named last changes fastest.
Arguments:
- query_raw: bfloat16 [32, 8, 256, 1536], P('tm', 'space', None, 'head'), may hold values from -40 to 40
- key_raw: bfloat16 [32, 8, 256, 1536], P('tm', 'space', None, 'head'), may hold values from -40 to 40
- values: bfloat16 [32, 8, 256, 1536], P('tm', 'space', None, 'head'), may hold values from -6 to 6
- out_grad: bfloat16 [32, 8, 256, 1536], P('tm', 'space', None, 'head'), may hold values from -192 to 192
- query_gain: float32 [128], replicated, may hold values from 0.1 to 1.9
- key_gain: float32 [128], replicated, may hold values from 0.1 to 1.9
- window_extent: int32 [12, 3], P('head'), may hold values from 0 to 1, as said below
- tile_counts: int32 [4, 8, 8], replicated, may hold values from 64 to 256, as said below
Outputs:
- query_raw_grad: bfloat16 [32, 8, 256, 1536], P('tm', 'space', None, 'head')
- key_raw_grad: bfloat16 [32, 8, 256, 1536], P('tm', 'space', None, 'head')
- value_grads: bfloat16 [32, 8, 256, 1536], P('tm', 'space', None, 'head')
- gain_grads: float32 [2, 128], replicated
Inputs may be any that keep to these rules, and one draw needn't show every extreme that they name: `window_extent`: each head's reaches (time, tile columns, tile rows) are (0, 0, 0), (1, 0, 0) or (0, 1, 1); in each of the 2 runs of 6 consecutive heads each of the three occurs exactly 6 // 3 times. `tile_counts`: tiles off the last time tile and off the last tile row are full.
All inputs are finite; a program needn't handle non-finite values.
Results may differ from a plain program's by a relative error of at most 0.009.
Values may be sent and summed in bfloat16 or wider, within the bound.
A program may use at most 64 MiB of HBM per device.

v0:
```python
import jax
import jax.numpy as jnp
from jax import lax
from jax.sharding import PartitionSpec as P

OFFSETS_BY_KIND = (
    ((0, 0, 0),),
    ((0, 0, 0), (-1, 0, 0), (1, 0, 0)),
    (
        (0, 0, 0),
        (0, -1, -1),
        (0, -1, 0),
        (0, -1, 1),
        (0, 0, -1),
        (0, 0, 1),
        (0, 1, -1),
        (0, 1, 0),
        (0, 1, 1),
    ),
)


def passed_along(x, axis, by):
    devices = lax.axis_size(axis)
    pairs = [(i, i + by) for i in range(devices) if 0 <= i + by < devices]
    return lax.ppermute(x, axis, pairs)


def padded(cells, sides, width):
    for axis, dim in sides:
        count = lax.axis_size(axis)
        ends = count - 1
        head = lax.slice_in_dim(cells, 0, width, axis=dim)
        tail = lax.slice_in_dim(cells, cells.shape[dim] - width, cells.shape[dim], axis=dim)
        cells = jnp.concatenate(
            [
                lax.ppermute(tail, axis, [(i, (i + 1) % count) for i in range(ends)]),
                cells,
                lax.ppermute(head, axis, [((i + 1) % count, i) for i in range(ends)]),
            ],
            axis=dim,
        )
    return cells


def product(pattern, left_op, right_op):
    return jnp.einsum(pattern, left_op, right_op, preferred_element_type=jnp.float32)


def normalize(raw_rows, gain_vec, head_count):
    row_count = raw_rows.shape[0]
    entries = raw_rows.astype(jnp.float32).reshape(row_count, head_count, -1)
    inverse = lax.rsqrt(jnp.mean(entries * entries, axis=2, keepdims=True) + 1e-06)
    unit_rows = entries * inverse
    normed = (unit_rows * gain_vec).astype(jnp.bfloat16)
    return (normed, unit_rows, inverse)


def norm_backward(upstream, unit_rows, inverse, gain_vec):
    scaled = upstream * gain_vec
    inner_mean = jnp.mean(scaled * unit_rows, axis=2, keepdims=True)
    return (inverse * (scaled - unit_rows * inner_mean), jnp.sum(upstream * unit_rows, axis=(0, 1)))


def key_mask(key_count, tile_len):
    return (jnp.arange(tile_len, dtype=jnp.int32) < key_count)[None, None, :]


def forward_stats(
    product, query_n, key_tiles, value_tiles, window_masks, query_ok, upstream, score_scale
):
    logits = [product("qhe,khe->hqk", query_n, key_tile) * score_scale for key_tile in key_tiles]
    totals = jnp.zeros(logits[0].shape[:2], jnp.float32)
    for logit_block, window_mask in zip(logits, window_masks):
        totals = totals + jnp.sum(jnp.where(window_mask, jnp.exp(logit_block), 0.0), axis=2)
    log_total = jnp.log(totals)
    row_mask = query_ok[None, :, None]
    weights = [
        jnp.where(window_mask & row_mask, jnp.exp(logit_block - log_total[:, :, None]), 0.0)
        for logit_block, window_mask in zip(logits, window_masks)
    ]
    weights_b = [weight_block.astype(jnp.bfloat16) for weight_block in weights]
    attended = jnp.zeros(query_n.shape, jnp.float32)
    for weight_b, value_tile in zip(weights_b, value_tiles):
        attended = attended + product("hqk,khe->qhe", weight_b, value_tile)
    out_dot = jnp.einsum("qhe,qhe->hq", upstream.astype(jnp.float32), attended)
    return (log_total, out_dot, weights, weights_b)


def query_grads(
    product, query_n, key_tiles, value_tiles, upstream, out_dot, weights, weights_b, score_scale
):
    query_grad = jnp.zeros(query_n.shape, jnp.float32)
    key_parts, value_parts = ([], [])
    for block_idx in range(len(key_tiles)):
        prob_grad = product("qhe,khe->hqk", upstream, value_tiles[block_idx])
        logit_grad = (weights[block_idx] * (prob_grad - out_dot[:, :, None])).astype(jnp.bfloat16)
        query_grad = (
            query_grad + product("hqk,khe->qhe", logit_grad, key_tiles[block_idx]) * score_scale
        )
        key_parts.append(product("hqk,qhe->khe", logit_grad, query_n) * score_scale)
        value_parts.append(product("hqk,qhe->khe", weights_b[block_idx], upstream))
    return (query_grad, key_parts, value_parts)


def tile_count(tile_counts, time_at, col_at, row_at):
    time_len, col_len, row_len = tile_counts.shape
    inside = (
        (time_at >= 0)
        & (time_at < time_len)
        & (col_at >= 0)
        & (col_at < col_len)
        & (row_at >= 0)
        & (row_at < row_len)
    )
    picked = tile_counts[
        jnp.clip(time_at, 0, time_len - 1),
        jnp.clip(col_at, 0, col_len - 1),
        jnp.clip(row_at, 0, row_len - 1),
    ]
    return jnp.where(inside, picked, 0)


def on_device(
    query_raw, key_raw, values, out_grad, query_gain, key_gain, window_extent, tile_counts
):
    tile_len = query_raw.shape[2]
    feat_width = query_raw.shape[3]
    local_heads = window_extent.shape[0]
    head_dim = feat_width // local_heads
    kind_size = local_heads // 3
    score_scale = head_dim ** (-0.5)
    col_count = lax.axis_size("tm") // tile_counts.shape[0]
    flat_pos = lax.axis_index("tm")
    time_pos = flat_pos // col_count
    col_pos = flat_pos % col_count
    row_pos = lax.axis_index("space")
    lanes_idx = jnp.arange(tile_len, dtype=jnp.int32)
    query_n, query_unit, query_inv = normalize(query_raw[0, 0], query_gain, local_heads)
    key_n, key_unit, key_inv = normalize(key_raw[0, 0], key_gain, local_heads)
    value_rows = values[0, 0].reshape(tile_len, local_heads, head_dim)
    upstream_rows = out_grad[0, 0].reshape(tile_len, local_heads, head_dim)
    kind_code = window_extent[:, 0] + 2 * window_extent[:, 1]
    head_order = jnp.argsort(kind_code * local_heads + jnp.arange(local_heads, dtype=jnp.int32))
    inverse = jnp.argsort(head_order)

    def select(rows, kind_idx):
        return jnp.take(rows, head_order[kind_idx * kind_size : (kind_idx + 1) * kind_size], axis=1)

    def count_at(offset):
        return tile_count(
            tile_counts, time_pos + offset[0], col_pos + offset[1], row_pos + offset[2]
        )

    own_count = count_at((0, 0, 0))
    query_ok = lanes_idx < own_count
    group_query = [select(query_n, kind_idx) for kind_idx in range(3)]
    group_key = [select(key_n, kind_idx) for kind_idx in range(3)]
    group_value = [select(value_rows, kind_idx) for kind_idx in range(3)]
    group_upstream = [select(upstream_rows, kind_idx) for kind_idx in range(3)]
    time_stack = jnp.stack([group_key[1], group_value[1]])
    time_near = {}
    for step_by in (col_count, -col_count):
        time_near[-step_by // col_count] = passed_along(time_stack, "tm", step_by)
    space_stack = jnp.stack([group_key[2], group_value[2]]).reshape(
        2, 1, 1, tile_len, kind_size * head_dim
    )
    row_rim = padded(space_stack, (("space", 2),), 1)
    side_rims = {}
    for col_shift in (-1, 1):
        side_rims[col_shift] = passed_along(row_rim, "tm", -col_shift)
    space_near = jnp.concatenate([side_rims[-1], row_rim, side_rims[1]], axis=1)

    def near_pair(kind_idx, offset):
        if offset == (0, 0, 0):
            return (group_key[kind_idx], group_value[kind_idx])
        if kind_idx == 1:
            fetched = time_near[offset[0]]
            return (fetched[0], fetched[1])
        fetched = space_near[:, 1 + offset[1], 1 + offset[2]].reshape(
            2, tile_len, kind_size, head_dim
        )
        return (fetched[0], fetched[1])

    query_acc, key_acc, value_acc, stats_group, key_terms, value_terms = ([], [], [], [], [], [])
    for kind_idx in range(3):
        offsets = OFFSETS_BY_KIND[kind_idx]
        tiles_near = [near_pair(kind_idx, offset) for offset in offsets]
        block_masks = [key_mask(count_at(offset), tile_len) for offset in offsets]
        part_count = len(offsets)
        grads_here, totals_here, dots_here = ([], [], [])
        parts_key = [[] for offset in offsets]
        parts_value = [[] for offset in offsets]
        for head_at in range(kind_size):
            single = slice(head_at, head_at + 1)
            key_tiles = [kv_pair[0][:, single] for kv_pair in tiles_near]
            value_tiles = [kv_pair[1][:, single] for kv_pair in tiles_near]
            log_total, out_dot, weights, weights_b = forward_stats(
                product,
                group_query[kind_idx][:, single],
                key_tiles,
                value_tiles,
                block_masks,
                query_ok,
                group_upstream[kind_idx][:, single],
                score_scale,
            )
            query_grad, key_parts, value_parts = query_grads(
                product,
                group_query[kind_idx][:, single],
                key_tiles,
                value_tiles,
                group_upstream[kind_idx][:, single],
                out_dot,
                weights,
                weights_b,
                score_scale,
            )
            grads_here.append(query_grad)
            totals_here.append(log_total)
            dots_here.append(out_dot)
            for block_idx in range(part_count):
                parts_key[block_idx].append(key_parts[block_idx])
                parts_value[block_idx].append(value_parts[block_idx])
        query_acc.append(jnp.concatenate(grads_here, axis=1))
        stats_group.append(
            jnp.stack([jnp.concatenate(totals_here, axis=0), jnp.concatenate(dots_here, axis=0)])
        )
        key_terms.append(
            {
                offsets[block_idx]: jnp.concatenate(parts_key[block_idx], axis=1)
                for block_idx in range(part_count)
            }
        )
        value_terms.append(
            {
                offsets[block_idx]: jnp.concatenate(parts_value[block_idx], axis=1)
                for block_idx in range(part_count)
            }
        )
        key_acc.append(key_terms[kind_idx][0, 0, 0])
        value_acc.append(value_terms[kind_idx][0, 0, 0])
    for time_shift in (-1, 1):
        payload = jnp.stack(
            [key_terms[1][time_shift, 0, 0], value_terms[1][time_shift, 0, 0]]
        ).astype(jnp.bfloat16)
        arrived = passed_along(payload, "tm", time_shift * col_count)
        key_acc[1] = key_acc[1] + arrived[0].astype(jnp.float32)
        value_acc[1] = value_acc[1] + arrived[1].astype(jnp.float32)
    column_arrivals = {}
    for col_shift in (-1, 1):
        payload = jnp.stack(
            [
                jnp.stack(
                    [key_terms[2][0, col_shift, row_shift], value_terms[2][0, col_shift, row_shift]]
                )
                for row_shift in (-1, 0, 1)
            ]
        ).astype(jnp.bfloat16)
        column_arrivals[col_shift] = passed_along(payload, "tm", col_shift)
    for col_shift in (-1, 1):
        key_acc[2] = key_acc[2] + column_arrivals[col_shift][1, 0].astype(jnp.float32)
        value_acc[2] = value_acc[2] + column_arrivals[col_shift][1, 1].astype(jnp.float32)
    for row_shift in (-1, 1):
        own_pair = jnp.stack(
            [key_terms[2][0, 0, row_shift], value_terms[2][0, 0, row_shift]]
        ).astype(jnp.bfloat16)
        payload = jnp.stack(
            [own_pair, column_arrivals[-1][row_shift + 1], column_arrivals[1][row_shift + 1]]
        )
        arrived = passed_along(payload, "space", row_shift)
        key_acc[2] = key_acc[2] + jnp.sum(arrived[:, 0].astype(jnp.float32), axis=0)
        value_acc[2] = value_acc[2] + jnp.sum(arrived[:, 1].astype(jnp.float32), axis=0)
    query_grad = jnp.take(jnp.concatenate(query_acc, axis=1), inverse, axis=1)
    key_grad = jnp.take(jnp.concatenate(key_acc, axis=1), inverse, axis=1)
    value_grad = jnp.take(jnp.concatenate(value_acc, axis=1), inverse, axis=1)
    query_back, query_gain_part = norm_backward(query_grad, query_unit, query_inv, query_gain)
    key_back, key_gain_part = norm_backward(key_grad, key_unit, key_inv, key_gain)
    gain_sums = lax.psum((query_gain_part, key_gain_part), ("tm", "space", "head"))
    gain_grads = jnp.stack([gain_sums[0], gain_sums[1]])
    shape_out = (1, 1, tile_len, feat_width)
    return (
        query_back.astype(jnp.bfloat16).reshape(shape_out),
        key_back.astype(jnp.bfloat16).reshape(shape_out),
        value_grad.astype(jnp.bfloat16).reshape(shape_out),
        gain_grads,
    )


def solution(mesh):
    placed = (
        P("tm", "space", None, "head"),
        P("tm", "space", None, "head"),
        P("tm", "space", None, "head"),
        P("tm", "space", None, "head"),
        P(),
        P(),
        P("head", None),
        P(),
    )
    return jax.shard_map(
        on_device,
        mesh=mesh,
        in_specs=placed,
        out_specs=(
            P("tm", "space", None, "head"),
            P("tm", "space", None, "head"),
            P("tm", "space", None, "head"),
            P(),
        ),
        check_vma=False,
    )
```

profile of v0, /device:TPU:1, one launch (start us, length us, event | category | flops | bytes accessed | tf_op | source)
XLA Modules:
  0.0 373.0 jit_solution(12087777012669063444)
XLA Ops:
  1.4 1.0 sort.31
  3.6 1.2 copy.88
  6.6 1.2 gather_fusion.11
  7.8 1.2 gather_fusion.2
  10.0 1.2 gather_fusion.9
  11.3 1.2 gather_fusion.1
  14.0 1.2 gather_fusion.8
  15.1 1.2 gather_fusion
  17.0 1.8 select_bitcast_fusion.1
  19.6 1.9 select_bitcast_fusion.2
  22.2 8.9 %collective-permute-start.3 = (bf16[2,1,1,256,256]{3,4,2,1,0:T(8,128)(2,1)}, bf16[2,1,1,256,256]{3,4,2,1,0:T(8,128)(2,1)}, u32[]{:S(2)}, u32[]{:S(2)}) collective-permute-start(bf16[2,1,1,256,256]{3,4,2,1,0:T(8,128)(2,1)} %pad_maximum_fusion.8), channel_id=1, source_target_pairs={{2,0},{4,2},{6,4},{8,6},{10,8},{12,10},{14,12},{3,1},{5,3},{7,5},{... | collective-permute-start | bytes 786440 | tf_op jit(solution)/shard_map/ppermute | solution.py:39
  31.1 1.9 collective-permute-start.2
  37.1 1.3 collective-permute-start.1
  38.4 13.4 %collective-permute-start = (bf16[2,256,2,128]{1,3,2,0:T(8,128)(2,1)}, bf16[2,256,2,128]{1,3,2,0:T(8,128)(2,1)}, u32[]{:S(2)}, u32[]{:S(2)}) collective-permute-start(bf16[2,256,2,128]{1,3,2,0:T(8,128)(2,1)} %pad_maximum_fusion.7), channel_id=1, source_target_pairs={{0,128},{16,144},{32,160},{48,176},{64,192},{80,208},{96,224},{112... | collective-permute-start | bytes 786440 | tf_op jit(solution)/shard_map/ppermute | solution.py:26
  52.4 1.0 sort.32
  54.4 1.2 gather_fusion.7
  57.1 0.9 convolution_multiply_fusion.25
  59.5 1.8 fusion.262
  63.4 2.0 select_reduce_fusion.8
  65.4 0.9 convolution_bitcast_fusion.5
  66.9 0.9 fusion.57
  78.7 1.7 copy.134
  82.5 0.9 convolution_bitcast_fusion.4
  84.0 0.9 fusion.56
  85.5 1.7 copy.166
  88.0 1.7 copy.146
  90.4 1.7 fusion.63
  92.1 1.0 slice_bitcast_fusion.8
  93.3 1.0 slice_bitcast_fusion.9
  105.9 1.1 pad_maximum_fusion
  107.1 1.3 collective-permute-start.5
  108.4 4.0 %collective-permute-start.4 = (bf16[2,1,3,256,256]{3,4,2,1,0:T(8,128)(2,1)S(1)}, bf16[2,1,3,256,256]{3,4,2,1,0:T(8,128)(2,1)S(1)}, u32[]{:S(2)}, u32[]{:S(2)}) collective-permute-start(bf16[2,1,3,256,256]{3,4,2,1,0:T(8,128)(2,1)S(1)} %pad_maximum_fusion), channel_id=1, source_target_pairs={{0,16},{16,32},{32,48},{48,64},{64,80},{80,96},{96,112},{112,128},... | collective-permute-start | bytes 2359304 | tf_op jit(solution)/shard_map/ppermute | solution.py:26
  112.4 1.0 fusion.260
  114.9 11.5 %collective-permute-start.7 = (bf16[2,256,2,128]{1,3,2,0:T(8,128)(2,1)S(1)}, bf16[2,256,2,128]{1,3,2,0:T(8,128)(2,1)S(1)}, u32[]{:S(2)}, u32[]{:S(2)}) collective-permute-start(bf16[2,256,2,128]{1,3,2,0:T(8,128)(2,1)S(1)} %pad_maximum_fusion.10), channel_id=1, source_target_pairs={{0,128},{16,144},{32,160},{48,176},{64,192},{80,208},{96,224},{112... | collective-permute-start | bytes 786440 | tf_op jit(solution)/shard_map/ppermute | solution.py:26
  126.5 1.5 collective-permute-start.6
  129.9 1.0 fusion.261
  131.8 1.0 collective-permute-done.7
  132.8 34.1 %collective-permute-done.6 = bf16[2,256,2,128]{1,3,2,0:T(8,128)(2,1)S(1)} collective-permute-done((bf16[2,256,2,128]{1,3,2,0:T(8,128)(2,1)S(1)}, bf16[2,256,2,128]{1,3,2,0:T(8,128)(2,1)S(1)}, u32[]{:S(2)}, u32[]{:S(2)}) %collective-permute-start.6) | collective-permute-done | bytes 262176 | tf_op jit(solution)/shard_map/ppermute | solution.py:26
  196.6 17.2 %collective-permute-start.9 = (bf16[3,2,256,2,128]{2,4,3,1,0:T(8,128)(2,1)S(1)}, bf16[3,2,256,2,128]{2,4,3,1,0:T(8,128)(2,1)S(1)}, u32[]{:S(2)}, u32[]{:S(2)}) collective-permute-start(bf16[3,2,256,2,128]{2,4,3,1,0:T(8,128)(2,1)S(1)} %pad_maximum_fusion.2), channel_id=1, source_target_pairs={{0,16},{16,32},{32,48},{48,64},{64,80},{80,96},{96,112},{112,128},... | collective-permute-start | bytes 2359304 | tf_op jit(solution)/shard_map/ppermute | solution.py:26
  214.1 1.5 collective-permute-start.8
  216.9 12.2 %collective-permute-done.9 = bf16[3,2,256,2,128]{2,4,3,1,0:T(8,128)(2,1)S(1)} collective-permute-done((bf16[3,2,256,2,128]{2,4,3,1,0:T(8,128)(2,1)S(1)}, bf16[3,2,256,2,128]{2,4,3,1,0:T(8,128)(2,1)S(1)}, u32[]{:S(2)}, u32[]{:S(2)}) %collective-permute-start.9) | collective-permute-done | bytes 786464 | tf_op jit(solution)/shard_map/ppermute | solution.py:26
  229.2 4.2 %collective-permute-done.8 = bf16[3,2,256,2,128]{2,4,3,1,0:T(8,128)(2,1)S(1)} collective-permute-done((bf16[3,2,256,2,128]{2,4,3,1,0:T(8,128)(2,1)S(1)}, bf16[3,2,256,2,128]{2,4,3,1,0:T(8,128)(2,1)S(1)}, u32[]{:S(2)}, u32[]{:S(2)}) %collective-permute-start.8) | collective-permute-done | bytes 786464 | tf_op jit(solution)/shard_map/ppermute | solution.py:26
  233.4 0.9 copy-done.16
  234.3 1.0 pad_maximum_fusion.4
  235.3 6.4 %collective-permute-start.11 = (bf16[3,2,256,2,128]{2,4,3,1,0:T(8,128)(2,1)}, bf16[3,2,256,2,128]{2,4,3,1,0:T(8,128)(2,1)}, u32[]{:S(2)}, u32[]{:S(2)}) collective-permute-start(bf16[3,2,256,2,128]{2,4,3,1,0:T(8,128)(2,1)} %pad_maximum_fusion.4), channel_id=1, source_target_pairs={{0,2},{2,4},{4,6},{6,8},{8,10},{10,12},{12,14},{1,3},{3,5},{5,7},{... | collective-permute-start | bytes 2359304 | tf_op jit(solution)/shard_map/ppermute | solution.py:26
  241.7 1.0 pad_maximum_fusion.3
  242.7 1.9 collective-permute-start.10
  245.4 1.9 gather_fusion.12
  247.3 0.9 fusion.52
  248.2 0.8 fusion.53
  249.6 1.3 collective-permute-done.11
  250.9 1.3 convert_reduce_fusion
  252.2 4.1 %collective-permute-done.10 = bf16[3,2,256,2,128]{2,4,3,1,0:T(8,128)(2,1)} collective-permute-done((bf16[3,2,256,2,128]{2,4,3,1,0:T(8,128)(2,1)}, bf16[3,2,256,2,128]{2,4,3,1,0:T(8,128)(2,1)}, u32[]{:S(2)}, u32[]{:S(2)}) %collective-permute-start.10) | collective-permute-done | bytes 786464 | tf_op jit(solution)/shard_map/ppermute | solution.py:26
  256.3 2.0 convert_reduce_fusion.1
  258.3 1.1 fusion.159
  260.3 0.9 copy.124
  261.3 1.2 fusion.155
  262.5 1.0 pad_maximum_fusion.5
  263.5 1.9 gather_fusion.13
  265.4 1.1 fusion.151
  267.2 1.0 multiply_convert_fusion
  268.2 0.9 copy.123
  269.2 0.9 copy.122
  270.7 101.6 %all-reduce = (f32[1,128]{1,0:T(1,128)S(1)}, f32[1,128]{1,0:T(1,128)S(1)}) all-reduce(f32[1,128]{1,0:T(1,128)S(1)} %bitcast.1024, f32[1,128]{1,0:T(1,128)S(1)} %bitcast.1023), channel_id=1, replica_groups=mesh['tm'=32,'space'=8,'head'=2] {'tm','space','head'}, use_global_device_ids=true, to_apply=%region_39.42 | all-reduce | flops 256 | bytes 2048 | tf_op jit(solution)/shard_map/psum | solution.py:279
  (412 shorter events, 79.2 us)
Async XLA Ops:
  5.0 1.2 copy-start.37
  6.5 2.5 copy-start.38
  10.0 2.4 copy-start.39
  19.6 1.9 copy-start.6
  22.2 10.8 %copy-start.78 = (s32[2]{0:T(128)S(1)}, s32[2]{0:T(128)}, u32[]{:S(2)}) copy-start(s32[2]{0:T(128)} %get-tuple-element.61) | copy-start | bytes 28
  22.2 83.1 %collective-permute-start.3 = (bf16[2,1,1,256,256]{3,4,2,1,0:T(8,128)(2,1)}, bf16[2,1,1,256,256]{3,4,2,1,0:T(8,128)(2,1)}, u32[]{:S(2)}, u32[]{:S(2)}) collective-permute-start(bf16[2,1,1,256,256]{3,4,2,1,0:T(8,128)(2,1)} %pad_maximum_fusion.8), channel_id=1, source_target_pairs={{2,0},{4,2},{6,4},{8,6},{10,8},{12,10},{14,12},{3,1},{5,3},{7,5},{... | collective-permute-start | bytes 786440 | tf_op jit(solution)/shard_map/ppermute | solution.py:39
  31.1 74.2 %collective-permute-start.2 = (bf16[2,1,1,256,256]{3,4,2,1,0:T(8,128)(2,1)}, bf16[2,1,1,256,256]{3,4,2,1,0:T(8,128)(2,1)}, u32[]{:S(2)}, u32[]{:S(2)}) collective-permute-start(bf16[2,1,1,256,256]{3,4,2,1,0:T(8,128)(2,1)} %pad_maximum_fusion.8), channel_id=1, source_target_pairs={{0,2},{2,4},{4,6},{6,8},{8,10},{10,12},{12,14},{1,3},{3,5},{5,7},{... | collective-permute-start | bytes 786440 | tf_op jit(solution)/shard_map/ppermute | solution.py:37
  36.3 19.5 %copy-start.8 = (bf16[256,2,128]{0,2,1:T(8,128)(2,1)}, bf16[256,2,128]{0,2,1:T(8,128)(2,1)S(1)}, u32[]{:S(2)}) copy-start(bf16[256,2,128]{0,2,1:T(8,128)(2,1)S(1)} %get-tuple-element.91) | copy-start | bytes 393220
  37.1 55.0 %collective-permute-start.1 = (bf16[2,256,2,128]{1,3,2,0:T(8,128)(2,1)}, bf16[2,256,2,128]{1,3,2,0:T(8,128)(2,1)}, u32[]{:S(2)}, u32[]{:S(2)}) collective-permute-start(bf16[2,256,2,128]{1,3,2,0:T(8,128)(2,1)} %pad_maximum_fusion.7), channel_id=1, source_target_pairs={{128,0},{144,16},{160,32},{176,48},{192,64},{208,80},{224,96},{240... | collective-permute-start | bytes 786440 | tf_op jit(solution)/shard_map/ppermute | solution.py:26
  38.4 55.0 %collective-permute-start = (bf16[2,256,2,128]{1,3,2,0:T(8,128)(2,1)}, bf16[2,256,2,128]{1,3,2,0:T(8,128)(2,1)}, u32[]{:S(2)}, u32[]{:S(2)}) collective-permute-start(bf16[2,256,2,128]{1,3,2,0:T(8,128)(2,1)} %pad_maximum_fusion.7), channel_id=1, source_target_pairs={{0,128},{16,144},{32,160},{48,176},{64,192},{80,208},{96,224},{112... | collective-permute-start | bytes 786440 | tf_op jit(solution)/shard_map/ppermute | solution.py:26
  55.9 0.9 copy-start.4
  55.9 1.0 copy-start.5
  57.1 6.3 %copy-start.11 = (f32[256,256]{0,1:T(8,128)}, f32[256,256]{0,1:T(8,128)S(1)}, u32[]{:S(2)}) copy-start(f32[256,256]{0,1:T(8,128)S(1)} %convolution_multiply_fusion.24) | copy-start | bytes 786436
  57.1 1.0 copy-start.17
  63.4 2.0 copy-start.13
  63.4 2.0 copy-start.18
  65.4 0.9 copy-start.43
  65.4 1.0 copy-start.45
  67.7 10.9 %copy-start.30 = (bf16[2,256,128]{2,1,0:T(8,128)(2,1)S(1)}, bf16[2,256,128]{2,1,0:T(8,128)(2,1)}, u32[]{:S(2)}) copy-start(bf16[2,256,128]{2,1,0:T(8,128)(2,1)} %gather_fusion.7) | copy-start | bytes 393220
  78.7 1.7 copy-start.1
  81.1 1.4 copy-start.12
  81.1 1.4 copy-start.19
  82.5 0.9 copy-start.44
  82.5 1.0 copy-start.46
  85.5 85.0 %copy-start.74 = (pred[256]{0:T(512)(128)(4,1)}, pred[256]{0:T(512)(128)(4,1)S(1)}, u32[]{:S(2)}) copy-start(pred[256]{0:T(512)(128)(4,1)S(1)} %iota_compare_fusion.1) | copy-start | bytes 772
  85.5 1.7 copy-start.24
  87.9 1.7 copy-start.23
  98.3 0.9 copy-start.36
  99.5 0.9 copy-start.35
  101.4 0.9 copy-start.9
  103.0 0.9 copy-start.34
  105.0 0.9 copy-start.7
  107.1 61.2 %collective-permute-start.5 = (bf16[2,1,3,256,256]{3,4,2,1,0:T(8,128)(2,1)S(1)}, bf16[2,1,3,256,256]{3,4,2,1,0:T(8,128)(2,1)S(1)}, u32[]{:S(2)}, u32[]{:S(2)}) collective-permute-start(bf16[2,1,3,256,256]{3,4,2,1,0:T(8,128)(2,1)S(1)} %pad_maximum_fusion), channel_id=1, source_target_pairs={{16,0},{32,16},{48,32},{64,48},{80,64},{96,80},{112,96},{128,112},... | collective-permute-start | bytes 2359304 | tf_op jit(solution)/shard_map/ppermute | solution.py:26
  108.4 60.6 %collective-permute-start.4 = (bf16[2,1,3,256,256]{3,4,2,1,0:T(8,128)(2,1)S(1)}, bf16[2,1,3,256,256]{3,4,2,1,0:T(8,128)(2,1)S(1)}, u32[]{:S(2)}, u32[]{:S(2)}) collective-permute-start(bf16[2,1,3,256,256]{3,4,2,1,0:T(8,128)(2,1)S(1)} %pad_maximum_fusion), channel_id=1, source_target_pairs={{0,16},{16,32},{32,48},{48,64},{64,80},{80,96},{96,112},{112,128},... | collective-permute-start | bytes 2359304 | tf_op jit(solution)/shard_map/ppermute | solution.py:26
  114.9 17.9 %collective-permute-start.7 = (bf16[2,256,2,128]{1,3,2,0:T(8,128)(2,1)S(1)}, bf16[2,256,2,128]{1,3,2,0:T(8,128)(2,1)S(1)}, u32[]{:S(2)}, u32[]{:S(2)}) collective-permute-start(bf16[2,256,2,128]{1,3,2,0:T(8,128)(2,1)S(1)} %pad_maximum_fusion.10), channel_id=1, source_target_pairs={{0,128},{16,144},{32,160},{48,176},{64,192},{80,208},{96,224},{112... | collective-permute-start | bytes 786440 | tf_op jit(solution)/shard_map/ppermute | solution.py:26
  126.4 1.5 copy-start.69
  126.5 40.4 %collective-permute-start.6 = (bf16[2,256,2,128]{1,3,2,0:T(8,128)(2,1)S(1)}, bf16[2,256,2,128]{1,3,2,0:T(8,128)(2,1)S(1)}, u32[]{:S(2)}, u32[]{:S(2)}) collective-permute-start(bf16[2,256,2,128]{1,3,2,0:T(8,128)(2,1)S(1)} %pad_maximum_fusion.9), channel_id=1, source_target_pairs={{128,0},{144,16},{160,32},{176,48},{192,64},{208,80},{224,96},{240... | collective-permute-start | bytes 786440 | tf_op jit(solution)/shard_map/ppermute | solution.py:26
  177.5 7.8 %copy-start.47 = (f32[256]{0:T(256)}, f32[256]{0:T(256)S(1)}, u32[]{:S(2)}) copy-start(f32[256]{0:T(256)S(1)} %add_log_fusion) | copy-start | bytes 3076
  179.5 0.9 copy-start.3
  182.1 0.9 copy-start.33
  185.5 6.7 %copy-start.26 = (bf16[256,256]{0,1:T(8,128)(2,1)}, bf16[256,256]{0,1:T(8,128)(2,1)S(1)}, u32[]{:S(2)}) copy-start(bf16[256,256]{0,1:T(8,128)(2,1)S(1)} %fusion.43) | copy-start | bytes 393220
  187.3 0.9 copy-start.32
  190.6 3.0 copy-start.28
  196.6 32.6 %collective-permute-start.9 = (bf16[3,2,256,2,128]{2,4,3,1,0:T(8,128)(2,1)S(1)}, bf16[3,2,256,2,128]{2,4,3,1,0:T(8,128)(2,1)S(1)}, u32[]{:S(2)}, u32[]{:S(2)}) collective-permute-start(bf16[3,2,256,2,128]{2,4,3,1,0:T(8,128)(2,1)S(1)} %pad_maximum_fusion.2), channel_id=1, source_target_pairs={{0,16},{16,32},{32,48},{48,64},{64,80},{80,96},{96,112},{112,128},... | collective-permute-start | bytes 2359304 | tf_op jit(solution)/shard_map/ppermute | solution.py:26
  214.1 19.2 %collective-permute-start.8 = (bf16[3,2,256,2,128]{2,4,3,1,0:T(8,128)(2,1)S(1)}, bf16[3,2,256,2,128]{2,4,3,1,0:T(8,128)(2,1)S(1)}, u32[]{:S(2)}, u32[]{:S(2)}) collective-permute-start(bf16[3,2,256,2,128]{2,4,3,1,0:T(8,128)(2,1)S(1)} %pad_maximum_fusion.1), channel_id=1, source_target_pairs={{16,0},{32,16},{48,32},{64,48},{80,64},{96,80},{112,96},{128,112},... | collective-permute-start | bytes 2359304 | tf_op jit(solution)/shard_map/ppermute | solution.py:26
  229.1 13.5 %copy-start.15 = (bf16[3,2,256,2,128]{2,4,3,1,0:T(8,128)(2,1)}, bf16[3,2,256,2,128]{2,4,3,1,0:T(8,128)(2,1)S(1)}, u32[]{:S(2)}) copy-start(bf16[3,2,256,2,128]{2,4,3,1,0:T(8,128)(2,1)S(1)} %collective-permute-done.9) | copy-start | bytes 2359300
  233.4 0.9 copy-start.16
  235.3 15.6 %collective-permute-start.11 = (bf16[3,2,256,2,128]{2,4,3,1,0:T(8,128)(2,1)}, bf16[3,2,256,2,128]{2,4,3,1,0:T(8,128)(2,1)}, u32[]{:S(2)}, u32[]{:S(2)}) collective-permute-start(bf16[3,2,256,2,128]{2,4,3,1,0:T(8,128)(2,1)} %pad_maximum_fusion.4), channel_id=1, source_target_pairs={{0,2},{2,4},{4,6},{6,8},{8,10},{10,12},{12,14},{1,3},{3,5},{5,7},{... | collective-permute-start | bytes 2359304 | tf_op jit(solution)/shard_map/ppermute | solution.py:26
  242.7 13.6 %collective-permute-start.10 = (bf16[3,2,256,2,128]{2,4,3,1,0:T(8,128)(2,1)}, bf16[3,2,256,2,128]{2,4,3,1,0:T(8,128)(2,1)}, u32[]{:S(2)}, u32[]{:S(2)}) collective-permute-start(bf16[3,2,256,2,128]{2,4,3,1,0:T(8,128)(2,1)} %pad_maximum_fusion.3), channel_id=1, source_target_pairs={{2,0},{4,2},{6,4},{8,6},{10,8},{12,10},{14,12},{3,1},{5,3},{7,5},{... | collective-permute-start | bytes 2359304 | tf_op jit(solution)/shard_map/ppermute | solution.py:26
  245.4 1.9 copy-start.27
  247.3 0.9 copy-start.29
  258.2 1.1 copy-start.25
  258.2 1.1 copy-start.49
  258.3 1.1 copy-start.50
  260.3 1.0 copy-start.10
  260.3 1.0 copy-start.22
  261.3 1.2 copy-start.14
  261.3 1.2 copy-start.20
  261.3 1.2 copy-start.21
  263.5 1.9 copy-start.41
  263.5 1.9 copy-start.53
  263.5 1.9 copy-start.55
  263.5 1.9 copy-start.61
  268.2 1.0 copy-start
  (30 other events, 20.0 us)
where the time goes:
time: 375 us; the launch traced here: 373 us
  blocking collectives  102 us (27%)
  starting transfers between devices  70.9 us (19%)
  waiting for transfers between devices  56.9 us (15%)
  local copies, waits for them, and re-layouts  54.6 us (15%)
  matrix products  46.3 us (12%)
  other arithmetic  33.2 us (9%)
  between operations  9.55 us (3%)
    psum x1, blocking collectives, on_device(): lax.psum((query_gain_part, key_gain_part), ('tm', 'space', 'head'))  102 us
    ppermute x10, starting transfers between devices, passed_along(): return lax.ppermute(x, axis, pairs)  60 us
    ppermute x10, waiting for transfers between devices, passed_along(): return lax.ppermute(x, axis, pairs)  56.9 us
    dot_general x156, matrix products, product(): jnp.einsum(pattern, left_op, right_op, preferred_element_type=jnp.float32)  46.3 us
    unnamed x175, local copies, waits for them, and re-layouts  31.3 us
    gather x13, local copies, waits for them, and re-layouts, select(): jnp.take(rows, head_order[kind_idx * kind_size:(kind_idx + 1) * kind_size...  11.4 us
    ppermute x1, starting transfers between devices, padded(): lax.ppermute(head, axis, [((i + 1) % count, i) for i in range(ends)])  8.91 us
  transfers between devices with their start and end apart: 12, of which 6 were waited for; matrix products, arithmetic and copies ran while one was open for 16% of the time, Pallas kernels for 0%

commit v1 on v0

v1 whole, which is shorter than its diff:
```python
import functools

import jax
import jax.numpy as jnp
from jax import lax
from jax.experimental import pallas as pl
from jax.experimental.pallas import tpu as pltpu
from jax.sharding import PartitionSpec as P

MESH = pl.DeviceIdType.MESH
HD = 128
F32 = jnp.float32
BF16 = jnp.bfloat16
SCALE = HD**-0.5
LOG2E = 1.4426950408889634
NT = (((1,), (1,)), ((), ()))
NN = (((1,), (0,)), ((), ()))
TN = (((0,), (0,)), ((), ()))

LOCAL, TIME, SPACE = 0, 2, 4


def dot(a, b, dims):
    return lax.dot_general(a, b, dims, preferred_element_type=F32)


def unit_of(raw):
    x = raw.astype(F32)
    inv = lax.rsqrt(jnp.mean(x * x, axis=1, keepdims=True) + 1e-6)
    return x * inv, inv


def fold(x):
    return jnp.sum(x.reshape(x.shape[0] // 8, 8, x.shape[1]), axis=0)


def kernel(
    T, C, R, H, tile, chunk,
    we, counts, qgain, kgain, qraw, kraw, vals, ograd,
    oq, ok, ov, og,
    hq, hk, hv, ho, qs, dos, kvl, kvt, kvs, pp, dd, stats, dqt, fk, fv,
    tacc, xout, xin, zout, zin, sacc, rowo, rowi, colo, coli,
    resq, resk, resv, gacc, gbuf,
    zf_s, zf_r, xf_s, xf_r, cf_s, cf_r, rf_s, rf_r,
    zb_s, zb_r, xb_s, xb_r, cb_s, cb_r, rb_s, rb_r, g_s, g_r,
):
    tm = lax.axis_index("tm")
    r = lax.axis_index("space")
    hd = lax.axis_index("head")
    t = lax.div(tm, C)
    c = lax.rem(tm, C)
    tz = t + 1 - 2 * lax.rem(t, 2)
    tx = lax.rem(t + 2, T)
    td = lax.rem(tz + 2, T)

    def dev(t_, c_, r_, h_):
        return (t_ * C + c_, r_, h_)

    G0 = T * H
    gi = t * H + hd

    def peer0(j):
        g = lax.rem(gi + j, G0)
        return dev(lax.div(g, H), c, r, lax.rem(g, H))

    def peer1(j):
        return dev(t, lax.rem(c + j, C), r, hd)

    def peer2(j):
        return dev(t, c, lax.rem(r + j, R), hd)

    groups = ((G0, gi, peer0), (C, c, peer1), (R, r, peer2))
    barrier = pltpu.get_barrier_semaphore()
    for size, _, peer in groups:
        for j in range(1, size):
            pl.semaphore_signal(barrier, inc=1, device_id=peer(j), device_id_type=MESH)

    kinds = [we[h, 0] + 2 * we[h, 1] for h in range(6)]
    head_of = []
    for kind in range(3):
        low, high = jnp.int32(5), jnp.int32(0)
        for h in range(6):
            low = jnp.minimum(low, jnp.where(kinds[h] == kind, h, 5))
            high = jnp.maximum(high, jnp.where(kinds[h] == kind, h, 0))
        head_of += [low, high]
    slot_of = []
    for h in range(6):
        before = jnp.int32(0)
        for g in range(h):
            before = before + jnp.where(kinds[g] == kinds[h], 1, 0)
        slot_of.append(2 * kinds[h] + before)

    for by_head, whole in ((hk, kraw), (hv, vals), (hq, qraw), (ho, ograd)):
        for h in range(6):
            by_head[h] = whole[:, h * HD : (h + 1) * HD]

    def raw(ref, slot):
        return ref[head_of[slot]]

    def normed(ref, slot, gain):
        unit, _ = unit_of(raw(ref, slot))
        return (unit * gain[...]).astype(BF16)

    def count_at(t_, c_, r_):
        inside = (c_ >= 0) & (c_ < C) & (r_ >= 0) & (r_ < R)
        got = counts[t_, lax.rem(c_ + C, C), lax.rem(r_ + R, R)]
        return jnp.where(inside, got, 0)

    own_count = count_at(t, c, r)
    lanes = lax.broadcasted_iota(jnp.int32, (1, tile), 1)
    query_ok = lanes < own_count
    rows_iota = lax.broadcasted_iota(jnp.int32, (chunk, tile), 0)

    def side(step):
        return (step + 1) // 2

    def c_ok(step):
        return (c + step >= 0) & (c + step < C)

    def r_ok(step):
        return (r + step >= 0) & (r + step < R)

    def c_dev(step):
        return dev(t, lax.rem(c + step + C, C), r, hd)

    def r_dev(step):
        return dev(t, c, lax.rem(r + step + R, R), hd)

    def copy(src, dst, send, recv, where):
        return pltpu.make_async_remote_copy(
            src_ref=src, dst_ref=dst, send_sem=send, recv_sem=recv, device_id=where, device_id_type=MESH
        )

    def col_fwd(step):
        return copy(kvs.at[1, 1], kvs.at[1, 1 - step], cf_s.at[side(step)], cf_r.at[side(-step)], c_dev(step))

    def row_fwd(step, dc):
        return copy(
            kvs.at[1, 1 + dc], kvs.at[1 - step, 1 + dc],
            rf_s.at[side(step), 1 + dc], rf_r.at[side(-step), 1 + dc], r_dev(step),
        )

    def z_fwd(h):
        return copy(kvt.at[0, h], kvt.at[1, h], zf_s.at[h], zf_r.at[h], dev(tz, c, r, hd))

    def x_fwd(h):
        return copy(kvt.at[1, h], kvt.at[2, h], xf_s.at[h], xf_r.at[h], dev(tx, c, r, hd))

    def x_bwd(h):
        return copy(xout.at[h], xin.at[h], xb_s.at[h], xb_r.at[h], dev(tx, c, r, hd))

    def z_bwd(h):
        return copy(zout.at[h], zin.at[h], zb_s.at[h], zb_r.at[h], dev(tz, c, r, hd))

    def row_bwd(step, h):
        return copy(
            rowo.at[h, side(step)], rowi.at[h, side(-step)],
            rb_s.at[h, side(step)], rb_r.at[h, side(-step)], r_dev(step),
        )

    def col_bwd(step, h):
        return copy(
            colo.at[h, side(step)], coli.at[h, side(-step)],
            cb_s.at[h, side(step)], cb_r.at[h, side(-step)], c_dev(step),
        )

    def on(condition, action):
        pl.when(condition)(action)

    STEPS = (-1, 1)

    for h in range(2):
        kvs[1, 1, h, 0] = normed(hk, SPACE + h, kgain)
        kvs[1, 1, h, 1] = raw(hv, SPACE + h)
    pl.semaphore_wait(barrier, G0 - 1 + C - 1 + R - 1)
    for step in STEPS:
        on(c_ok(step), col_fwd(step).start)
    for step in STEPS:
        on(r_ok(step), row_fwd(step, 0).start)
    for h in range(2):
        kvt[0, h, 0] = normed(hk, TIME + h, kgain)
        kvt[0, h, 1] = raw(hv, TIME + h)
        z_fwd(h).start()

    nothing = jnp.zeros((2, 2, tile, HD), BF16)
    for step in STEPS:

        def blank_column(step=step):
            for dr in range(3):
                kvs[dr, 1 + step] = nothing

        def blank_row(step=step):
            for dc in range(3):
                kvs[1 + step, dc] = nothing

        on(jnp.logical_not(c_ok(step)), blank_column)
        on(jnp.logical_not(r_ok(step)), blank_row)

    for h in range(2):
        kvl[h, 0] = normed(hk, LOCAL + h, kgain)
        kvl[h, 1] = raw(hv, LOCAL + h)
    for s in range(6):
        qs[s] = normed(hq, s, qgain)
        dos[s] = raw(ho, s)
    stats[...] = jnp.zeros_like(stats)
    dqt[...] = jnp.zeros_like(dqt)
    gacc[...] = jnp.zeros_like(gacc)
    sacc[...] = jnp.zeros_like(sacc)

    def pass_one(idx, slot, kv, count):
        query, up = qs[slot], dos[slot]
        sum_l, sum_d = stats[slot, 0:8], stats[slot, 8:16]
        for j in range(0, tile, chunk):
            s = dot(kv[0, j : j + chunk], query, NT)
            p = jnp.where(rows_iota < count - j, jnp.exp2(s * (SCALE * LOG2E)), 0.0)
            dp = dot(kv[1, j : j + chunk], up, NT)
            pp[idx, j : j + chunk] = p
            dd[idx, j : j + chunk] = dp
            sum_l = sum_l + fold(p)
            sum_d = sum_d + fold(p * dp)
        stats[slot, 0:8] = sum_l
        stats[slot, 8:16] = sum_d

    def finish_stats(slot):
        inv = 1.0 / jnp.sum(stats[slot, 0:8], axis=0, keepdims=True)
        out_dot = jnp.sum(stats[slot, 8:16], axis=0, keepdims=True) * inv
        stats[slot, 0:8] = jnp.broadcast_to(jnp.where(query_ok, inv, 0.0), (8, tile))
        stats[slot, 8:16] = jnp.broadcast_to(out_dot, (8, tile))

    def pass_two(idx, slot, kv, emit):
        query, up = qs[slot], dos[slot]
        inv, out_dot = stats[slot, 0:1], stats[slot, 8:9]
        key_sum = gacc[slot]
        dq = dqt[slot]
        for j in range(0, tile, chunk):
            w = pp[idx, j : j + chunk] * inv
            g = (w * (dd[idx, j : j + chunk] - out_dot)).astype(BF16)
            keys = kv[0, j : j + chunk]
            dk = dot(g, query, NN)
            dv = dot(w.astype(BF16), up, NN)
            dq = dq + dot(keys, g, TN)
            key_sum = key_sum + fold(dk * keys.astype(F32))
            emit(j, dk, dv)
        gacc[slot] = key_sum
        dqt[slot] = dq

    def at_time(h, b):
        return 2 + 3 * h + b

    def at_space(h, dr, dc):
        return 8 + 9 * h + 3 * dr + dc

    def space_one(dr, dc):
        count = count_at(t, c + dc - 1, r + dr - 1)
        for h in range(2):
            pass_one(at_space(h, dr, dc), SPACE + h, kvs.at[dr, dc, h], count)

    def loop(n, body):
        def step(i, carry):
            body(i)
            return carry

        lax.fori_loop(0, n, step, 0)

    space_one(1, 1)
    for h in range(2):
        pass_one(h, LOCAL + h, kvl.at[h], own_count)
        finish_stats(LOCAL + h)
    for h in range(2):

        def emit_local(j, dk, dv, h=h):
            fk[LOCAL + h, j : j + chunk] = dk
            fv[LOCAL + h, j : j + chunk] = dv

        pass_two(h, LOCAL + h, kvl.at[h], emit_local)
    for h in range(2):
        pass_one(at_time(h, 0), TIME + h, kvt.at[0, h], own_count)

    for dc in STEPS:
        on(c_ok(dc), col_fwd(-dc).wait_recv)
    for dc in STEPS:
        for step in STEPS:
            on(c_ok(dc) & r_ok(step), row_fwd(step, dc).start)
    loop(2, lambda i: space_one(1, 2 * i))
    for dr in STEPS:
        on(r_ok(dr), row_fwd(-dr, 0).wait_recv)
    loop(2, lambda i: space_one(2 * i, 1))

    z_fwd(0).wait_recv()
    x_fwd(0).start()

    for dr in STEPS:
        for dc in STEPS:
            on(r_ok(dr) & c_ok(dc), row_fwd(-dr, dc).wait_recv)

    def corner(i):
        dr = lax.div(i, 2)
        space_one(2 * dr, 2 * (i - 2 * dr))

    loop(4, corner)
    for h in range(2):
        finish_stats(SPACE + h)

    for h in range(2):

        def outer_rows(i, h=h):
            d = lax.div(i, 3)
            dc = i - 3 * d

            def emit(j, dk, dv):
                rowo[h, d, dc, 0, pl.ds(j, chunk)] = dk.astype(BF16)
                rowo[h, d, dc, 1, pl.ds(j, chunk)] = dv.astype(BF16)

            pass_two(at_space(h, 2 * d, dc), SPACE + h, kvs.at[2 * d, dc, h], emit)

        loop(6, outer_rows)
        for step in STEPS:
            on(r_ok(step), row_bwd(step, h).start)

    time_counts = (own_count, count_at(tz, c, r), jnp.where((td - t) * (td - t) == 1, count_at(td, c, r), 0))

    def time_head(h):
        pass_one(at_time(h, 1), TIME + h, kvt.at[1, h], time_counts[1])
        x_fwd(h).wait_recv()
        pass_one(at_time(h, 2), TIME + h, kvt.at[2, h], time_counts[2])
        finish_stats(TIME + h)

        def emit_far(j, dk, dv):
            xout[h, 0, j : j + chunk] = dk.astype(BF16)
            xout[h, 1, j : j + chunk] = dv.astype(BF16)

        def emit_near(j, dk, dv):
            tacc[h, 0, j : j + chunk] = dk
            tacc[h, 1, j : j + chunk] = dv

        def emit_own(j, dk, dv):
            fk[TIME + h, j : j + chunk] = dk
            fv[TIME + h, j : j + chunk] = dv

        pass_two(at_time(h, 2), TIME + h, kvt.at[2, h], emit_far)
        x_bwd(h).start()
        pass_two(at_time(h, 1), TIME + h, kvt.at[1, h], emit_near)
        pass_two(at_time(h, 0), TIME + h, kvt.at[0, h], emit_own)
        x_bwd(h).wait_recv()
        zout[h] = (tacc[h] + xin[h].astype(F32)).astype(BF16)
        z_bwd(h).start()

    time_head(0)

    def middle_row(i):
        for h in range(2):

            def emit(j, dk, dv, h=h):
                sacc[i, h, 0, pl.ds(j, chunk)] = dk
                sacc[i, h, 1, pl.ds(j, chunk)] = dv

            pass_two(at_space(h, 1, i), SPACE + h, kvs.at[1, i, h], emit)

    loop(3, middle_row)

    z_fwd(1).wait_recv()
    x_fwd(1).start()

    for h in range(2):
        for dr in STEPS:

            def add_row(dr=dr, h=h):
                row_bwd(-dr, h).wait_recv()
                for dc in range(3):
                    sacc[dc, h] = sacc[dc, h] + rowi[h, side(dr), dc].astype(F32)

            on(r_ok(dr), add_row)
        for step in STEPS:

            def send_column(step=step, h=h):
                colo[h, side(step)] = sacc[1 + step, h].astype(BF16)
                col_bwd(step, h).start()

            on(c_ok(step), send_column)

    time_head(1)

    query_sum = jnp.zeros((8, HD), F32)
    for s in range(6):
        grad = jnp.transpose(dqt[s]) * SCALE
        unit, inv = unit_of(raw(hq, s))
        scaled = grad * qgain[...]
        mean = jnp.mean(scaled * unit, axis=1, keepdims=True)
        resq[s] = (inv * (scaled - unit * mean)).astype(BF16)
        query_sum = query_sum + fold(grad * unit)
    key_sum = gacc[0]
    for s in range(1, 6):
        key_sum = key_sum + gacc[s]

    def gain_copy(n, j):
        _, mine, peer = groups[n]
        return copy(gbuf.at[n, mine], gbuf.at[n, mine], g_s.at[n, j], g_r.at[n, mine], peer(j))

    def gain_send(n, value):
        size, mine, _ = groups[n]
        gbuf[n, mine] = value
        for j in range(1, size):
            gain_copy(n, j).start()

    def gain_sum(n):
        size, mine, peer = groups[n]
        for j in range(1, size):
            other = lax.rem(mine + j, size)
            copy(gbuf.at[n, other], gbuf.at[n, other], g_s.at[n, j], g_r.at[n, other], peer(j)).wait_recv()
        total = gbuf[n, 0]
        for i in range(1, size):
            total = total + gbuf[n, i]
        return total

    pair = jnp.concatenate(
        [
            jnp.sum(query_sum, axis=0, keepdims=True),
            jnp.sum(key_sum, axis=0, keepdims=True) * SCALE / kgain[...],
            jnp.zeros((6, HD), F32),
        ],
        axis=0,
    )
    gain_send(0, pair)

    def key_out(s):
        grad = fk[s] * SCALE
        unit, inv = unit_of(raw(hk, s))
        scaled = grad * kgain[...]
        mean = jnp.mean(scaled * unit, axis=1, keepdims=True)
        resk[s] = (inv * (scaled - unit * mean)).astype(BF16)
        resv[s] = fv[s].astype(BF16)

    for h in range(2):
        key_out(LOCAL + h)
    gain_send(1, gain_sum(0))

    for h in range(6):
        oq[:, h * HD : (h + 1) * HD] = resq[slot_of[h]]
    for h in range(2):
        for dc in STEPS:

            def add_column(dc=dc, h=h):
                col_bwd(-dc, h).wait_recv()
                sacc[1, h] = sacc[1, h] + coli[h, side(dc)].astype(F32)

            on(c_ok(dc), add_column)
        fk[SPACE + h] = sacc[1, h, 0]
        fv[SPACE + h] = sacc[1, h, 1]
        key_out(SPACE + h)
    gain_send(2, gain_sum(1))

    for h in range(2):
        z_bwd(h).wait_recv()
        fk[TIME + h] = fk[TIME + h] + zin[h, 0].astype(F32)
        fv[TIME + h] = fv[TIME + h] + zin[h, 1].astype(F32)
        key_out(TIME + h)
    for h in range(6):
        ok[:, h * HD : (h + 1) * HD] = resk[slot_of[h]]
        ov[:, h * HD : (h + 1) * HD] = resv[slot_of[h]]
    og[...] = gain_sum(2)[0:2]

    for h in range(2):
        z_fwd(h).wait_send()
        x_fwd(h).wait_send()
        x_bwd(h).wait_send()
        z_bwd(h).wait_send()
    for step in STEPS:
        on(c_ok(step), col_fwd(step).wait_send)
        on(r_ok(step), row_fwd(step, 0).wait_send)
        for dc in STEPS:
            on(c_ok(dc) & r_ok(step), row_fwd(step, dc).wait_send)
        for h in range(2):
            on(r_ok(step), row_bwd(step, h).wait_send)
            on(c_ok(step), col_bwd(step, h).wait_send)
    for n, (size, _, _) in enumerate(groups):
        for j in range(1, size):
            gain_copy(n, j).wait_send()


def on_device(T, C, R, H, query_raw, key_raw, values, out_grad, query_gain, key_gain, window_extent, tile_counts):
    tile, width = query_raw.shape[2], query_raw.shape[3]
    chunk = min(128, tile)
    flat = lambda x: x.reshape(tile, width)
    most = max(T * H, C, R)
    dma = pltpu.SemaphoreType.DMA
    vmem = pl.BlockSpec(memory_space=pltpu.VMEM)
    smem = pl.BlockSpec(memory_space=pltpu.SMEM)
    blocks = 2 + 6 + 18
    scratch = [
        pltpu.VMEM((6, tile, HD), BF16),
        pltpu.VMEM((6, tile, HD), BF16),
        pltpu.VMEM((6, tile, HD), BF16),
        pltpu.VMEM((6, tile, HD), BF16),
        pltpu.VMEM((6, tile, HD), BF16),
        pltpu.VMEM((6, tile, HD), BF16),
        pltpu.VMEM((2, 2, tile, HD), BF16),
        pltpu.VMEM((3, 2, 2, tile, HD), BF16),
        pltpu.VMEM((3, 3, 2, 2, tile, HD), BF16),
        pltpu.VMEM((blocks, tile, tile), F32),
        pltpu.VMEM((blocks, tile, tile), F32),
        pltpu.VMEM((6, 16, tile), F32),
        pltpu.VMEM((6, HD, tile), F32),
        pltpu.VMEM((6, tile, HD), F32),
        pltpu.VMEM((6, tile, HD), F32),
        pltpu.VMEM((2, 2, tile, HD), F32),
        pltpu.VMEM((2, 2, tile, HD), BF16),
        pltpu.VMEM((2, 2, tile, HD), BF16),
        pltpu.VMEM((2, 2, tile, HD), BF16),
        pltpu.VMEM((2, 2, tile, HD), BF16),
        pltpu.VMEM((3, 2, 2, tile, HD), F32),
        pltpu.VMEM((2, 2, 3, 2, tile, HD), BF16),
        pltpu.VMEM((2, 2, 3, 2, tile, HD), BF16),
        pltpu.VMEM((2, 2, 2, tile, HD), BF16),
        pltpu.VMEM((2, 2, 2, tile, HD), BF16),
        pltpu.VMEM((6, tile, HD), BF16),
        pltpu.VMEM((6, tile, HD), BF16),
        pltpu.VMEM((6, tile, HD), BF16),
        pltpu.VMEM((6, 8, HD), F32),
        pltpu.VMEM((3, most, 8, HD), F32),
        dma((2,)), dma((2,)), dma((2,)), dma((2,)),
        dma((2,)), dma((2,)), dma((2, 3)), dma((2, 3)),
        dma((2,)), dma((2,)), dma((2,)), dma((2,)),
        dma((2, 2)), dma((2, 2)), dma((2, 2)), dma((2, 2)),
        dma((3, most)), dma((3, most)),
    ]
    wide = jax.ShapeDtypeStruct((tile, width), BF16)
    grad_q, grad_k, grad_v, gains = pl.pallas_call(
        functools.partial(kernel, T, C, R, H, tile, chunk),
        out_shape=(wide, wide, wide, jax.ShapeDtypeStruct((2, HD), F32)),
        in_specs=[smem, smem] + [vmem] * 6,
        out_specs=(vmem,) * 4,
        scratch_shapes=scratch,
        compiler_params=pltpu.CompilerParams(
            collective_id=0, has_side_effects=True, vmem_limit_bytes=60 * 1024 * 1024
        ),
    )(
        window_extent,
        tile_counts,
        query_gain.reshape(1, HD),
        key_gain.reshape(1, HD),
        flat(query_raw),
        flat(key_raw),
        flat(values),
        flat(out_grad),
    )
    shape = (1, 1, tile, width)
    return grad_q.reshape(shape), grad_k.reshape(shape), grad_v.reshape(shape), gains


def solution(mesh):
    tile_spec = P("tm", "space", None, "head")

    def program(*args):
        T = args[7].shape[0]
        C = mesh.shape["tm"] // T
        return on_device(T, C, mesh.shape["space"], mesh.shape["head"], *args)

    return jax.shard_map(
        program,
        mesh=mesh,
        in_specs=(tile_spec,) * 4 + (P(), P(), P("head", None), P()),
        out_specs=(tile_spec,) * 3 + (P(),),
        check_vma=False,
    )
```

time: 375 us -> 109 us (0.29)
  Pallas kernels: 0 us -> 102 us
  blocking collectives: 102 us -> 0 us
  starting transfers between devices: 70.9 us -> 0 us
  waiting for transfers between devices: 56.9 us -> 0 us
  local copies, waits for them, and re-layouts: 54.6 us -> 5.62 us
  matrix products: 46.3 us -> 0 us
  other arithmetic: 33.2 us -> 0 us
  between operations: 9.55 us -> 0.66 us
    pallas_call x0 -> x1, Pallas kernels: none -> 102 us  [on_device(): pl.pallas_call(functools.partial(kernel, T, C, R, H, tile, chunk), out_sh...]
    psum x1 -> x0, blocking collectives: 102 us -> none  [on_device(): lax.psum((query_gain_part, key_gain_part), ('tm', 'space', 'head'))]
    ppermute x12 -> x0, starting transfers between devices: 70.9 us -> none  [the longest x10 60 us: passed_along(): return lax.ppermute(x, axis, pairs)]
    ppermute x12 -> x0, waiting for transfers between devices: 56.9 us -> none  [the longest x10 56.9 us: passed_along(): return lax.ppermute(x, axis, pairs)]
    dot_general x156 -> x0, matrix products: 46.3 us -> none  [product(): jnp.einsum(pattern, left_op, right_op, preferred_element_type=jnp.float32)]
    unnamed x175 -> x13, local copies, waits for them, and re-layouts: 31.3 us -> 5.62 us
    gather x16 -> x0, local copies, waits for them, and re-layouts: 15.9 us -> none  [the longest x13 11.4 us: select(): jnp.take(rows, head_order[kind_idx * kind_size:(kind_idx + 1) * kind_size...]
    another operation x36 -> x0, other arithmetic: 5.47 us -> none  [the longest x2 1.95 us: on_device(): jnp.stack([own_pair, column_arrivals[-1][row_shift + 1], column_arrivals[...]
  transfers between devices with their start and end apart: 12 -> 0, of which waited for: 6 -> 0; matrix products, arithmetic and copies ran while one was open for 16% -> 0% of each run, Pallas kernels for 0% -> 0%
where the time goes in v1:
time: 109 us
  Pallas kernels  102 us (94%)
  local copies, waits for them, and re-layouts  5.62 us (5%)
    pallas_call x1, Pallas kernels, on_device(): pl.pallas_call(functools.partial(kernel, T, C, R, H, tile, chunk), out_sh...  102 us
    unnamed x13, local copies, waits for them, and re-layouts  5.62 us

profile of v1, /device:TPU:1, one launch (start us, length us, event | category | flops | bytes accessed | tf_op | source)
XLA Modules:
  0.0 108.5 jit_solution(10647685180092287303)
XLA Ops:
  0.6 0.0 copy-start.2
  0.6 0.7 copy-done.2
  1.3 0.7 copy.12.we
  2.0 102.2 %shard_map.111 = (bf16[256,768]{1,0:T(8,128)(2,1)}, bf16[256,768]{1,0:T(8,128)(2,1)}, bf16[256,768]{1,0:T(8,128)(2,1)}, f32[2,128]{1,0:T(2,128)}) custom-call(s32[6,3]{1,0:T(8,128)} %copy.12.we, s32[4,8,8]{2,1,0:T(8,128)} %counts.1, f32[1,128]{1,0:T(1,128)} %bitcast.16, f32[1,128]{1,0:T(1,128)} %bitcast.17, bf16[256,768]{1,0:T(8,128)(2,1)} %bitcast.12, ...), custom_call_target="tpu_custom_call" | custom-call | tf_op jit(solution)/shard_map/pallas_call | solution.py:527
  104.2 0.0 copy-start.1
  104.2 1.8 %copy.17 = bf16[1,1,256,768]{3,2,1,0:T(8,128)(2,1)} copy(bf16[1,1,256,768]{3,2,1,0:T(8,128)(2,1)} %bitcast.11) | data formatting | bytes 786432
  106.1 0.0 copy-done.1
  106.1 0.0 copy-start
  106.1 0.7 copy.18
  106.8 0.4 copy-done
  107.2 0.0 copy-start.3
  107.2 0.7 copy.19
  107.9 0.0 copy-done.3
  107.9 0.6 copy.20
Async XLA Ops:
  0.6 0.7 copy-start.2
  104.2 1.8 %copy-start.1 = (bf16[256,768]{1,0:T(8,128)(2,1)S(1)}, bf16[256,768]{1,0:T(8,128)(2,1)}, u32[]{:S(2)}) copy-start(bf16[256,768]{1,0:T(8,128)(2,1)} %get-tuple-element.9) | copy-start | bytes 1179652
  106.1 1.1 %copy-start = (bf16[256,768]{1,0:T(8,128)(2,1)S(1)}, bf16[256,768]{1,0:T(8,128)(2,1)}, u32[]{:S(2)}) copy-start(bf16[256,768]{1,0:T(8,128)(2,1)} %get-tuple-element.10) | copy-start | bytes 1179652
  107.2 0.8 copy-start.3

commit v2 on v1

v2 whole, which is shorter than its diff:
```python
import functools

import jax
import jax.numpy as jnp
from jax import lax
from jax.experimental import pallas as pl
from jax.experimental.pallas import tpu as pltpu
from jax.sharding import PartitionSpec as P

MESH = pl.DeviceIdType.MESH
HD = 128
F32 = jnp.float32
BF16 = jnp.bfloat16
SCALE = HD**-0.5
LOG2E = 1.4426950408889634
NT = (((1,), (1,)), ((), ()))
NN = (((1,), (0,)), ((), ()))
TN = (((0,), (0,)), ((), ()))

LOCAL, TIME, SPACE = 0, 2, 4


def dot(a, b, dims):
    return lax.dot_general(a, b, dims, preferred_element_type=F32)


def unit_of(raw):
    x = raw.astype(F32)
    inv = lax.rsqrt(jnp.mean(x * x, axis=1, keepdims=True) + 1e-6)
    return x * inv, inv


def fold(x):
    return jnp.sum(x.reshape(x.shape[0] // 8, 8, x.shape[1]), axis=0)


def kernel(
    T, C, R, H, tile, chunk,
    we, counts, qgain, kgain, qraw, kraw, vals, ograd,
    oq, ok, ov, og,
    hq, hk, hv, ho, qs, kvl, kvh, qdt, kvs, pp, dd, stats, sto, sti, dqt, fk, fv,
    xout, xin, zout, zin, sacc, rowo, rowi, colo, coli, gacc, gbuf,
    zf_s, zf_r, xf_s, xf_r, cf_s, cf_r, rf_s, rf_r,
    zb_s, zb_r, xb_s, xb_r, cb_s, cb_r, rb_s, rb_r, st_s, st_r, g_s, g_r,
):
    tm = lax.axis_index("tm")
    r = lax.axis_index("space")
    hd = lax.axis_index("head")
    t = lax.div(tm, C)
    c = lax.rem(tm, C)
    tz = t + 1 - 2 * lax.rem(t, 2)
    tx = lax.rem(t + 2, T)
    td = lax.rem(tz + 2, T)

    def dev(t_, c_, r_, h_):
        return (t_ * C + c_, r_, h_)

    G0 = T * H
    gi = t * H + hd

    def peer0(j):
        g = lax.rem(gi + j, G0)
        return dev(lax.div(g, H), c, r, lax.rem(g, H))

    def peer1(j):
        return dev(t, lax.rem(c + j, C), r, hd)

    def peer2(j):
        return dev(t, c, lax.rem(r + j, R), hd)

    groups = ((G0, gi, peer0), (C, c, peer1), (R, r, peer2))
    barrier = pltpu.get_barrier_semaphore()
    for size, _, peer in groups:
        for j in range(1, size):
            pl.semaphore_signal(barrier, inc=1, device_id=peer(j), device_id_type=MESH)

    kinds = [we[0, h] + 2 * we[1, h] for h in range(6)]
    head_of = []
    for kind in range(3):
        low, high = jnp.int32(5), jnp.int32(0)
        for h in range(6):
            low = jnp.minimum(low, jnp.where(kinds[h] == kind, h, 5))
            high = jnp.maximum(high, jnp.where(kinds[h] == kind, h, 0))
        head_of += [low, high]
    for by_head, whole in ((hk, kraw), (hv, vals), (hq, qraw), (ho, ograd)):
        for h in range(6):
            by_head[h] = whole[:, h * HD : (h + 1) * HD]

    def raw(ref, slot):
        return ref[head_of[slot]]

    def normed(ref, slot, gain):
        unit, _ = unit_of(raw(ref, slot))
        return (unit * gain[...]).astype(BF16)

    def count_at(t_, c_, r_):
        inside = (c_ >= 0) & (c_ < C) & (r_ >= 0) & (r_ < R)
        got = counts[t_, lax.rem(c_ + C, C), lax.rem(r_ + R, R)]
        return jnp.where(inside, got, 0)

    own_count = count_at(t, c, r)
    lanes = lax.broadcasted_iota(jnp.int32, (1, tile), 1)
    query_ok = lanes < own_count
    rows_iota = lax.broadcasted_iota(jnp.int32, (chunk, tile), 0)

    def side(step):
        return (step + 1) // 2

    def c_ok(step):
        return (c + step >= 0) & (c + step < C)

    def r_ok(step):
        return (r + step >= 0) & (r + step < R)

    def c_dev(step):
        return dev(t, lax.rem(c + step + C, C), r, hd)

    def r_dev(step):
        return dev(t, c, lax.rem(r + step + R, R), hd)

    def copy(src, dst, send, recv, where):
        return pltpu.make_async_remote_copy(
            src_ref=src, dst_ref=dst, send_sem=send, recv_sem=recv, device_id=where, device_id_type=MESH
        )

    def col_fwd(step):
        return copy(kvs.at[1, 1], kvs.at[1, 1 - step], cf_s.at[side(step)], cf_r.at[side(-step)], c_dev(step))

    def row_fwd(step, dc):
        return copy(
            kvs.at[1, 1 + dc], kvs.at[1 - step, 1 + dc],
            rf_s.at[side(step), 1 + dc], rf_r.at[side(-step), 1 + dc], r_dev(step),
        )

    def z_fwd(h):
        return copy(qdt.at[0, h], qdt.at[1, h], zf_s.at[h], zf_r.at[h], dev(tz, c, r, hd))

    def x_fwd(h):
        return copy(qdt.at[1, h], qdt.at[2, h], xf_s.at[h], xf_r.at[h], dev(tx, c, r, hd))

    def x_bwd(h):
        return copy(xout.at[h], xin.at[h], xb_s.at[h], xb_r.at[h], dev(tx, c, r, hd))

    def z_bwd(h):
        return copy(zout.at[h], zin.at[h], zb_s.at[h], zb_r.at[h], dev(tz, c, r, hd))

    def row_bwd(step, h):
        return copy(
            rowo.at[h, side(step)], rowi.at[h, side(-step)],
            rb_s.at[h, side(step)], rb_r.at[h, side(-step)], r_dev(step),
        )

    def col_bwd(step, h):
        return copy(
            colo.at[h, side(step)], coli.at[h, side(-step)],
            cb_s.at[h, side(step)], cb_r.at[h, side(-step)], c_dev(step),
        )

    def on(condition, action):
        pl.when(condition)(action)

    others = (tz, tx, td)

    def stat_copy(h, n):
        return copy(sto.at[h], sti.at[h, n], st_s.at[h, n], st_r.at[h, n], dev(others[n], c, r, hd))

    STEPS = (-1, 1)

    for h in range(2):
        kvs[1, 1, h, 0] = normed(hk, SPACE + h, kgain)
        kvs[1, 1, h, 1] = raw(hv, SPACE + h)
    pl.semaphore_wait(barrier, G0 - 1 + C - 1 + R - 1)
    for step in STEPS:
        on(c_ok(step), col_fwd(step).start)
    for step in STEPS:
        on(r_ok(step), row_fwd(step, 0).start)
    for h in range(2):
        qdt[0, h, 0] = normed(hq, TIME + h, qgain)
        qdt[0, h, 1] = raw(ho, TIME + h)
        if h == 0:
            z_fwd(0).start()

    nothing = jnp.zeros((2, 2, tile, HD), BF16)
    for step in STEPS:

        def blank_column(step=step):
            for dr in range(3):
                kvs[dr, 1 + step] = nothing

        def blank_row(step=step):
            for dc in range(3):
                kvs[1 + step, dc] = nothing

        on(jnp.logical_not(c_ok(step)), blank_column)
        on(jnp.logical_not(r_ok(step)), blank_row)

    for h in range(2):
        kvl[h, 0] = normed(hk, LOCAL + h, kgain)
        kvl[h, 1] = raw(hv, LOCAL + h)
        kvh[h, 0] = normed(hk, TIME + h, kgain)
        kvh[h, 1] = raw(hv, TIME + h)
        for n, s in ((0, LOCAL + h), (2, SPACE + h)):
            qs[n + h, 0] = normed(hq, s, qgain)
            qs[n + h, 1] = raw(ho, s)
    stats[...] = jnp.zeros_like(stats)
    dqt[...] = jnp.zeros_like(dqt)
    gacc[...] = jnp.zeros_like(gacc)

    def at_time(h, b):
        return 4 + 3 * h + b

    def pass_one(idx, row, qd, kv, count):
        query, up = qd[0], qd[1]
        sum_l, sum_d = stats[row, 0:8], stats[row, 8:16]
        for j in range(0, tile, chunk):
            s = dot(kv[0, j : j + chunk], query, NT)
            p = jnp.where(rows_iota < count - j, jnp.exp2(s * (SCALE * LOG2E)), 0.0)
            dp = dot(kv[1, j : j + chunk], up, NT)
            pp[idx, j : j + chunk] = p
            dd[idx, j : j + chunk] = dp
            sum_l = sum_l + fold(p)
            sum_d = sum_d + fold(p * dp)
        stats[row, 0:8] = sum_l
        stats[row, 8:16] = sum_d

    def put_stats(row, total, dot_total, ok_lanes):
        inv = 1.0 / total
        stats[row, 0:8] = jnp.broadcast_to(jnp.where(ok_lanes, inv, 0.0), (8, tile))
        stats[row, 8:16] = jnp.broadcast_to(dot_total * inv, (8, tile))

    def partial(row):
        total = jnp.sum(stats[row, 0:8], axis=0, keepdims=True)
        return total, jnp.sum(stats[row, 8:16], axis=0, keepdims=True)

    def finish_stats(row):
        put_stats(row, *partial(row), query_ok)

    def pass_two(idx, row, qd, kv, slot, emit):
        query, up = qd[0], qd[1]
        inv, out_dot = stats[row, 0:1], stats[row, 8:9]
        key_sum = gacc[slot]
        dq = dqt[row]
        for j in range(0, tile, chunk):
            w = pp[idx, j : j + chunk] * inv
            g = (w * (dd[idx, j : j + chunk] - out_dot)).astype(BF16)
            keys = kv[0, j : j + chunk]
            dk = dot(g, query, NN)
            dv = dot(w.astype(BF16), up, NN)
            dq = dq + dot(keys, g, TN)
            key_sum = key_sum + fold(dk * keys.astype(F32))
            emit(j, dk, dv)
        gacc[slot] = key_sum
        dqt[row] = dq

    def at_space(h, dr, dc):
        return 10 + 9 * h + 3 * dr + dc

    def space_one(dr, dc):
        count = count_at(t, c + dc - 1, r + dr - 1)
        for h in range(2):
            pass_one(at_space(h, dr, dc), 2 + h, qs.at[2 + h], kvs.at[dr, dc, h], count)

    def space_two(dr, dc, h, emit):
        pass_two(at_space(h, dr, dc), 2 + h, qs.at[2 + h], kvs.at[dr, dc, h], SPACE + h, emit)

    far_count = jnp.where((td - t) * (td - t) == 1, own_count, 0)
    tile_ok = (query_ok, lanes < count_at(tz, c, r), lanes < count_at(td, c, r))

    def time_one(h, b):
        pass_one(at_time(h, b), at_time(h, b), qdt.at[b, h], kvh.at[h], far_count if b == 2 else own_count)

    def time_two(h, b):
        def emit(j, dk, dv):
            if b == 2:
                fk[TIME + h, j : j + chunk] = dk
                fv[TIME + h, j : j + chunk] = dv
            else:
                fk[TIME + h, j : j + chunk] += dk
                fv[TIME + h, j : j + chunk] += dv

        pass_two(at_time(h, b), at_time(h, b), qdt.at[b, h], kvh.at[h], TIME + h, emit)

    def time_partial(h):
        for b in range(3):
            total, dot_total = partial(at_time(h, b))
            sto[h, 2 * b : 2 * b + 1] = total
            sto[h, 2 * b + 1 : 2 * b + 2] = dot_total
        sto[h, 6:8] = jnp.zeros((2, tile), F32)
        for n in range(3):
            stat_copy(h, n).start()

    def time_total(h):
        for n in range(3):
            stat_copy(h, n).wait_recv()
        for b, (n, i), (m, k) in ((0, (0, 2), (2, 4)), (1, (0, 0), (1, 4)), (2, (2, 0), (1, 2))):

            def row(q, b=b, n=n, i=i, m=m, k=k):
                mine = sto[h, 2 * b + q : 2 * b + q + 1]
                return mine + sti[h, n, i + q : i + q + 1] + sti[h, m, k + q : k + q + 1]

            put_stats(at_time(h, b), row(0), row(1), tile_ok[b])

    def time_send_far(h):
        time_two(h, 2)
        xout[h] = dqt[at_time(h, 2)].astype(BF16)
        x_bwd(h).start()

    def time_send_back(h):
        x_bwd(h).wait_recv()
        zout[h] = (dqt[at_time(h, 1)] + xin[h].astype(F32)).astype(BF16)
        z_bwd(h).start()

    def loop(n, body):
        def step(i, carry):
            body(i)
            return carry

        lax.fori_loop(0, n, step, 0)

    def query_out(s, grad_t):
        grad = jnp.transpose(grad_t) * SCALE
        unit, inv = unit_of(raw(hq, s))
        scaled = grad * qgain[...]
        mean = jnp.mean(scaled * unit, axis=1, keepdims=True)
        oq[s] = (inv * (scaled - unit * mean)).astype(BF16)

    def key_out(s):
        grad = fk[s] * SCALE
        unit, inv = unit_of(raw(hk, s))
        scaled = grad * kgain[...]
        mean = jnp.mean(scaled * unit, axis=1, keepdims=True)
        ok[s] = (inv * (scaled - unit * mean)).astype(BF16)
        ov[s] = fv[s].astype(BF16)

    space_one(1, 1)
    for h in range(2):
        pass_one(h, h, qs.at[h], kvl.at[h], own_count)
        finish_stats(h)
    for h in range(2):

        def emit_local(j, dk, dv, h=h):
            fk[LOCAL + h, j : j + chunk] = dk
            fv[LOCAL + h, j : j + chunk] = dv

        pass_two(h, h, qs.at[h], kvl.at[h], LOCAL + h, emit_local)
    for h in range(2):
        time_one(h, 0)

    for dc in STEPS:
        on(c_ok(dc), col_fwd(-dc).wait_recv)
    for dc in STEPS:
        for step in STEPS:
            on(c_ok(dc) & r_ok(step), row_fwd(step, dc).start)
    loop(2, lambda i: space_one(1, 2 * i))
    for dr in STEPS:
        on(r_ok(dr), row_fwd(-dr, 0).wait_recv)
    z_fwd(0).wait_send()
    z_fwd(1).start()
    loop(2, lambda i: space_one(2 * i, 1))

    z_fwd(0).wait_recv()
    x_fwd(0).start()
    time_one(0, 1)
    for dr in STEPS:
        for dc in STEPS:
            on(r_ok(dr) & c_ok(dc), row_fwd(-dr, dc).wait_recv)

    def corner(i):
        dr = lax.div(i, 2)
        space_one(2 * dr, 2 * (i - 2 * dr))

    loop(4, corner)
    x_fwd(0).wait_recv()
    time_one(0, 2)
    time_partial(0)
    for h in range(2):
        finish_stats(2 + h)

    def outer_rows(h):
        def step(i):
            d = lax.div(i, 3)
            dc = i - 3 * d

            def emit(j, dk, dv):
                rowo[h, d, dc, 0, pl.ds(j, chunk)] = dk.astype(BF16)
                rowo[h, d, dc, 1, pl.ds(j, chunk)] = dv.astype(BF16)

            space_two(2 * d, dc, h, emit)

        loop(6, step)
        for step in STEPS:
            on(r_ok(step), row_bwd(step, h).start)

    outer_rows(0)
    time_total(0)
    time_send_far(0)
    time_two(0, 1)
    outer_rows(1)
    time_send_back(0)

    def middle_row(i):
        for h in range(2):

            def emit(j, dk, dv, h=h):
                sacc[i, h, 0, pl.ds(j, chunk)] = dk
                sacc[i, h, 1, pl.ds(j, chunk)] = dv

            space_two(1, i, h, emit)

    loop(3, middle_row)
    time_two(0, 0)
    for h in range(2):
        query_out(LOCAL + h, dqt[h])
        query_out(SPACE + h, dqt[2 + h])
        key_out(LOCAL + h)
    key_out(TIME)

    z_fwd(1).wait_recv()
    x_fwd(1).start()
    time_one(1, 1)
    x_fwd(1).wait_recv()
    time_one(1, 2)
    time_partial(1)

    def rows_back(h):
        for dr in STEPS:

            def add_row(dr=dr):
                row_bwd(-dr, h).wait_recv()
                for dc in range(3):
                    sacc[dc, h] = sacc[dc, h] + rowi[h, side(dr), dc].astype(F32)

            on(r_ok(dr), add_row)
        for step in STEPS:

            def send_column(step=step):
                colo[h, side(step)] = sacc[1 + step, h].astype(BF16)
                col_bwd(step, h).start()

            on(c_ok(step), send_column)

    for h in range(2):
        rows_back(h)

    time_total(1)
    time_send_far(1)
    time_two(1, 1)
    time_two(1, 0)
    time_send_back(1)

    pair_sum = gacc[0]
    for s in range(1, 6):
        pair_sum = pair_sum + gacc[s]

    def gain_copy(n, j):
        _, mine, peer = groups[n]
        return copy(gbuf.at[n, mine], gbuf.at[n, mine], g_s.at[n, j], g_r.at[n, mine], peer(j))

    def gain_send(n, value):
        size, mine, _ = groups[n]
        gbuf[n, mine] = value
        for j in range(1, size):
            gain_copy(n, j).start()

    def gain_sum(n):
        size, mine, peer = groups[n]
        for j in range(1, size):
            other = lax.rem(mine + j, size)
            copy(gbuf.at[n, other], gbuf.at[n, other], g_s.at[n, j], g_r.at[n, other], peer(j)).wait_recv()
        total = gbuf[n, 0]
        for i in range(1, size):
            total = total + gbuf[n, i]
        return total

    gain_send(0, pair_sum)
    key_out(TIME + 1)
    for h in range(2):
        for dc in STEPS:

            def add_column(dc=dc, h=h):
                col_bwd(-dc, h).wait_recv()
                sacc[1, h] = sacc[1, h] + coli[h, side(dc)].astype(F32)

            on(c_ok(dc), add_column)
        fk[SPACE + h] = sacc[1, h, 0]
        fv[SPACE + h] = sacc[1, h, 1]
        key_out(SPACE + h)
        if h == 0:
            gain_send(1, gain_sum(0))
    gain_send(2, gain_sum(1))
    for h in range(2):
        z_bwd(h).wait_recv()
        query_out(TIME + h, dqt[at_time(h, 0)] + zin[h].astype(F32))
    total = jnp.sum(gain_sum(2), axis=0, keepdims=True) * SCALE
    og[...] = jnp.concatenate([total / qgain[...], total / kgain[...]], axis=0)

    z_fwd(1).wait_send()
    for h in range(2):
        x_fwd(h).wait_send()
        x_bwd(h).wait_send()
        z_bwd(h).wait_send()
        for n in range(3):
            stat_copy(h, n).wait_send()
    for step in STEPS:
        on(c_ok(step), col_fwd(step).wait_send)
        on(r_ok(step), row_fwd(step, 0).wait_send)
        for dc in STEPS:
            on(c_ok(dc) & r_ok(step), row_fwd(step, dc).wait_send)
        for h in range(2):
            on(r_ok(step), row_bwd(step, h).wait_send)
            on(c_ok(step), col_bwd(step, h).wait_send)
    for n, (size, _, _) in enumerate(groups):
        for j in range(1, size):
            gain_copy(n, j).wait_send()


def hand_over(we, q, k, v, gains, oq, ok, ov, og):
    kinds = [we[0, h] + 2 * we[1, h] for h in range(6)]
    for h in range(6):
        slot = 2 * kinds[h]
        for g in range(h):
            slot = slot + jnp.where(kinds[g] == kinds[h], 1, 0)
        for src, dst in ((q, oq), (k, ok), (v, ov)):
            dst[:, h * HD : (h + 1) * HD] = src[slot]
    og[...] = gains[...]


def on_device(T, C, R, H, query_raw, key_raw, values, out_grad, query_gain, key_gain, window_extent, tile_counts):
    tile, width = query_raw.shape[2], query_raw.shape[3]
    chunk = min(128, tile)
    flat = lambda x: x.reshape(tile, width)
    most = max(T * H, C, R)
    dma = pltpu.SemaphoreType.DMA
    vmem = pl.BlockSpec(memory_space=pltpu.VMEM)
    smem = pl.BlockSpec(memory_space=pltpu.SMEM)
    heads = lambda n: pltpu.VMEM((n, tile, HD), BF16)
    pairs = lambda *n: pltpu.VMEM(n + (2, tile, HD), BF16)
    scratch = [
        heads(6), heads(6), heads(6), heads(6),
        pairs(4), pairs(2), pairs(2), pairs(3, 2), pairs(3, 3, 2),
        pltpu.VMEM((28, tile, tile), F32),
        pltpu.VMEM((28, tile, tile), F32),
        pltpu.VMEM((10, 16, tile), F32),
        pltpu.VMEM((2, 8, tile), F32),
        pltpu.VMEM((2, 3, 8, tile), F32),
        pltpu.VMEM((10, HD, tile), F32),
        pltpu.VMEM((6, tile, HD), F32),
        pltpu.VMEM((6, tile, HD), F32),
        pltpu.VMEM((2, HD, tile), BF16),
        pltpu.VMEM((2, HD, tile), BF16),
        pltpu.VMEM((2, HD, tile), BF16),
        pltpu.VMEM((2, HD, tile), BF16),
        pltpu.VMEM((3, 2, 2, tile, HD), F32),
        pairs(2, 2, 3), pairs(2, 2, 3), pairs(2, 2), pairs(2, 2),
        pltpu.VMEM((6, 8, HD), F32),
        pltpu.VMEM((3, most, 8, HD), F32),
        dma((2,)), dma((2,)), dma((2,)), dma((2,)),
        dma((2,)), dma((2,)), dma((2, 3)), dma((2, 3)),
        dma((2,)), dma((2,)), dma((2,)), dma((2,)),
        dma((2, 2)), dma((2, 2)), dma((2, 2)), dma((2, 2)),
        dma((2, 3)), dma((2, 3)),
        dma((3, most)), dma((3, most)),
    ]
    wide = jax.ShapeDtypeStruct((6, tile, HD), BF16)
    extent = window_extent.T
    grad_q, grad_k, grad_v, gains = pl.pallas_call(
        functools.partial(kernel, T, C, R, H, tile, chunk),
        out_shape=(wide, wide, wide, jax.ShapeDtypeStruct((2, HD), F32)),
        in_specs=[smem, smem] + [vmem] * 6,
        out_specs=(vmem,) * 4,
        scratch_shapes=scratch,
        compiler_params=pltpu.CompilerParams(
            collective_id=0, has_side_effects=True, vmem_limit_bytes=60 * 1024 * 1024
        ),
    )(
        extent,
        tile_counts,
        query_gain.reshape(1, HD),
        key_gain.reshape(1, HD),
        flat(query_raw),
        flat(key_raw),
        flat(values),
        flat(out_grad),
    )
    whole = jax.ShapeDtypeStruct((tile, width), BF16)
    outs = pl.pallas_call(
        hand_over,
        out_shape=(whole, whole, whole, jax.ShapeDtypeStruct((2, HD), F32)),
        in_specs=[smem] + [vmem] * 4,
        out_specs=(vmem,) * 4,
        compiler_params=pltpu.CompilerParams(vmem_limit_bytes=60 * 1024 * 1024),
    )(extent, grad_q, grad_k, grad_v, gains)
    shape = (1, 1, tile, width)
    return tuple(x.reshape(shape) for x in outs[:3]) + (outs[3],)


def solution(mesh):
    tile_spec = P("tm", "space", None, "head")

    def program(*args):
        T = args[7].shape[0]
        C = mesh.shape["tm"] // T
        return on_device(T, C, mesh.shape["space"], mesh.shape["head"], *args)

    return jax.shard_map(
        program,
        mesh=mesh,
        in_specs=(tile_spec,) * 4 + (P(), P(), P("head", None), P()),
        out_specs=(tile_spec,) * 3 + (P(),),
        check_vma=False,
    )
```

time: 109 us -> 111 us (1.018)
  Pallas kernels: 102 us -> 111 us
  local copies, waits for them, and re-layouts: 5.62 us -> 0 us
    pallas_call x1, Pallas kernels: 102 us -> 108 us  [on_device(): pl.pallas_call(functools.partial(kernel, T, C, R, H, tile, chunk), out_sh...]
    unnamed x13 -> x0, local copies, waits for them, and re-layouts: 5.62 us -> none
    pallas_call x0 -> x1, Pallas kernels: none -> 2.47 us  [on_device(): pl.pallas_call(hand_over, out_shape=(whole, whole, whole, jax.ShapeDtypeS...]
where the time goes in v2:
time: 111 us
  Pallas kernels  111 us (100%)
    pallas_call x1, Pallas kernels, on_device(): pl.pallas_call(functools.partial(kernel, T, C, R, H, tile, chunk), out_sh...  108 us
    pallas_call x1, Pallas kernels, on_device(): pl.pallas_call(hand_over, out_shape=(whole, whole, whole, jax.ShapeDtypeS...  2.47 us

profile of v2, /device:TPU:1, one launch (start us, length us, event | category | flops | bytes accessed | tf_op | source)
XLA Modules:
  0.0 111.3 jit_solution(11822783017122498329)
XLA Ops:
  0.6 108.2 %shard_map.111 = (bf16[6,256,128]{2,1,0:T(8,128)(2,1)}, bf16[6,256,128]{2,1,0:T(8,128)(2,1)}, bf16[6,256,128]{2,1,0:T(8,128)(2,1)}, f32[2,128]{1,0:T(2,128)}) custom-call(s32[3,6]{1,0:T(4,128)} %bitcast.14, s32[4,8,8]{2,1,0:T(8,128)} %counts.1, f32[1,128]{1,0:T(1,128)} %bitcast.16, f32[1,128]{1,0:T(1,128)} %bitcast.17, bf16[256,768]{1,0:T(8,128)(2,1)} %bitcast.10, ...), custom_call_target="tpu_custom_call" | custom-call | tf_op jit(solution)/shard_map/pallas_call | solution.py:566
  108.8 2.5 %shard_map.112 = (bf16[256,768]{1,0:T(8,128)(2,1)}, bf16[256,768]{1,0:T(8,128)(2,1)}, bf16[256,768]{1,0:T(8,128)(2,1)}, f32[2,128]{1,0:T(2,128)}) custom-call(s32[3,6]{1,0:T(4,128)} %bitcast.15, bf16[6,256,128]{2,1,0:T(8,128)(2,1)} %get-tuple-element.12.q, bf16[6,256,128]{2,1,0:T(8,128)(2,1)} %get-tuple-element.13.k, ...), custom_call_target="tpu_custom_call" | custom-call | tf_op jit(solution)/shard_map/pallas_call | solution.py:586

commit v3 on v2

--- a/solution.py
+++ b/solution.py
@@ -39,9 +39,9 @@
     we, counts, qgain, kgain, qraw, kraw, vals, ograd,
     oq, ok, ov, og,
     hq, hk, hv, ho, qs, kvl, kvh, qdt, kvs, pp, dd, stats, sto, sti, dqt, fk, fv,
-    xout, xin, zout, zin, sacc, rowo, rowi, colo, coli, gacc, gbuf,
-    zf_s, zf_r, xf_s, xf_r, cf_s, cf_r, rf_s, rf_r,
-    zb_s, zb_r, xb_s, xb_r, cb_s, cb_r, rb_s, rb_r, st_s, st_r, g_s, g_r,
+    xout, xin, zout, zin, rly, rlb, sacc, rowo, rowi, colo, coli, gacc, gbuf,
+    z1_s, z1_r, z2_s, z2_r, xf_s, xf_r, cf_s, cf_r, rf_s, rf_r,
+    y1_s, y1_r, y2_s, y2_r, xb_s, xb_r, cb_s, cb_r, rb_s, rb_r, st_s, st_r, g_s, g_r,
 ):
     tm = lax.axis_index("tm")
     r = lax.axis_index("space")
@@ -69,7 +69,16 @@
         return dev(t, c, lax.rem(r + j, R), hd)
 
     groups = ((G0, gi, peer0), (C, c, peer1), (R, r, peer2))
+    near_half, far_half = C // 2, C - C // 2
+
+    def ring(offset):
+        place = lax.rem(lax.rem(t, 2) * C + c + offset + 2 * C, 2 * C)
+        return (lax.div(t, 2) * (2 * C) + place, r, hd)
+
+    relays = sorted({near_half, -near_half, far_half, -far_half})
     barrier = pltpu.get_barrier_semaphore()
+    for offset in relays:
+        pl.semaphore_signal(barrier, inc=1, device_id=ring(offset), device_id_type=MESH)
     for size, _, peer in groups:
         for j in range(1, size):
             pl.semaphore_signal(barrier, inc=1, device_id=peer(j), device_id_type=MESH)
@@ -132,17 +141,36 @@
             rf_s.at[side(step), 1 + dc], rf_r.at[side(-step), 1 + dc], r_dev(step),
         )
 
-    def z_fwd(h):
-        return copy(qdt.at[0, h], qdt.at[1, h], zf_s.at[h], zf_r.at[h], dev(tz, c, r, hd))
+    def z_first(h, n):
+        return copy(qdt.at[0, h, n], rly.at[h, n], z1_s.at[h, n], z1_r.at[h, n], ring((1 - 2 * n) * near_half))
+
+    def z_second(h, n):
+        return copy(rly.at[h, n], qdt.at[1, h, n], z2_s.at[h, n], z2_r.at[h, n], ring((1 - 2 * n) * far_half))
+
+    def back_first(h, n):
+        return copy(zout.at[h, n], rlb.at[h, n], y1_s.at[h, n], y1_r.at[h, n], ring((1 - 2 * n) * near_half))
+
+    def back_second(h, n):
+        return copy(rlb.at[h, n], zin.at[h, n], y2_s.at[h, n], y2_r.at[h, n], ring((1 - 2 * n) * far_half))
+
+    def begin(hop, h):
+        for n in range(2):
+            hop(h, n).start()
+
+    def arrived(hop, h):
+        for n in range(2):
+            hop(h, n).wait_recv()
+
+    def relay(first, second, h):
+        for n in range(2):
+            first(h, n).wait_recv()
+            second(h, n).start()
 
     def x_fwd(h):
         return copy(qdt.at[1, h], qdt.at[2, h], xf_s.at[h], xf_r.at[h], dev(tx, c, r, hd))
 
     def x_bwd(h):
         return copy(xout.at[h], xin.at[h], xb_s.at[h], xb_r.at[h], dev(tx, c, r, hd))
-
-    def z_bwd(h):
-        return copy(zout.at[h], zin.at[h], zb_s.at[h], zb_r.at[h], dev(tz, c, r, hd))
 
     def row_bwd(step, h):
         return copy(
@@ -169,7 +197,7 @@
     for h in range(2):
         kvs[1, 1, h, 0] = normed(hk, SPACE + h, kgain)
         kvs[1, 1, h, 1] = raw(hv, SPACE + h)
-    pl.semaphore_wait(barrier, G0 - 1 + C - 1 + R - 1)
+    pl.semaphore_wait(barrier, len(relays) + G0 - 1 + C - 1 + R - 1)
     for step in STEPS:
         on(c_ok(step), col_fwd(step).start)
     for step in STEPS:
@@ -178,7 +206,7 @@
         qdt[0, h, 0] = normed(hq, TIME + h, qgain)
         qdt[0, h, 1] = raw(ho, TIME + h)
         if h == 0:
-            z_fwd(0).start()
+            begin(z_first, 0)
 
     nothing = jnp.zeros((2, 2, tile, HD), BF16)
     for step in STEPS:
@@ -307,8 +335,10 @@
 
     def time_send_back(h):
         x_bwd(h).wait_recv()
-        zout[h] = (dqt[at_time(h, 1)] + xin[h].astype(F32)).astype(BF16)
-        z_bwd(h).start()
+        back = (dqt[at_time(h, 1)] + xin[h].astype(F32)).astype(BF16)
+        for n in range(2):
+            zout[h, n] = back[n * (HD // 2) : (n + 1) * (HD // 2)]
+        begin(back_first, h)
 
     def loop(n, body):
         def step(i, carry):
@@ -336,6 +366,8 @@
     for h in range(2):
         pass_one(h, h, qs.at[h], kvl.at[h], own_count)
         finish_stats(h)
+    relay(z_first, z_second, 0)
+    begin(z_first, 1)
     for h in range(2):
 
         def emit_local(j, dk, dv, h=h):
@@ -354,11 +386,10 @@
     loop(2, lambda i: space_one(1, 2 * i))
     for dr in STEPS:
         on(r_ok(dr), row_fwd(-dr, 0).wait_recv)
-    z_fwd(0).wait_send()
-    z_fwd(1).start()
     loop(2, lambda i: space_one(2 * i, 1))
-
-    z_fwd(0).wait_recv()
+    relay(z_first, z_second, 1)
+
+    arrived(z_second, 0)
     x_fwd(0).start()
     time_one(0, 1)
     for dr in STEPS:
@@ -395,8 +426,15 @@
     time_total(0)
     time_send_far(0)
     time_two(0, 1)
+
+    arrived(z_second, 1)
+    x_fwd(1).start()
+    time_one(1, 1)
+    time_send_back(0)
     outer_rows(1)
-    time_send_back(0)
+    x_fwd(1).wait_recv()
+    time_one(1, 2)
+    time_partial(1)
 
     def middle_row(i):
         for h in range(2):
@@ -409,18 +447,11 @@
 
     loop(3, middle_row)
     time_two(0, 0)
-    for h in range(2):
-        query_out(LOCAL + h, dqt[h])
-        query_out(SPACE + h, dqt[2 + h])
-        key_out(LOCAL + h)
-    key_out(TIME)
-
-    z_fwd(1).wait_recv()
-    x_fwd(1).start()
-    time_one(1, 1)
-    x_fwd(1).wait_recv()
-    time_one(1, 2)
-    time_partial(1)
+    relay(back_first, back_second, 0)
+    time_total(1)
+    time_send_far(1)
+    time_two(1, 1)
+    time_send_back(1)
 
     def rows_back(h):
         for dr in STEPS:
@@ -442,11 +473,7 @@
     for h in range(2):
         rows_back(h)
 
-    time_total(1)
-    time_send_far(1)
-    time_two(1, 1)
     time_two(1, 0)
-    time_send_back(1)
 
     pair_sum = gacc[0]
     for s in range(1, 6):
@@ -473,7 +500,13 @@
         return total
 
     gain_send(0, pair_sum)
-    key_out(TIME + 1)
+    for h in range(2):
+        query_out(LOCAL + h, dqt[h])
+        query_out(SPACE + h, dqt[2 + h])
+        key_out(LOCAL + h)
+    relay(back_first, back_second, 1)
+    for h in range(2):
+        key_out(TIME + h)
     for h in range(2):
         for dc in STEPS:
 
@@ -489,16 +522,17 @@
             gain_send(1, gain_sum(0))
     gain_send(2, gain_sum(1))
     for h in range(2):
-        z_bwd(h).wait_recv()
-        query_out(TIME + h, dqt[at_time(h, 0)] + zin[h].astype(F32))
+        arrived(back_second, h)
+        query_out(TIME + h, dqt[at_time(h, 0)] + jnp.concatenate([zin[h, 0], zin[h, 1]], axis=0).astype(F32))
     total = jnp.sum(gain_sum(2), axis=0, keepdims=True) * SCALE
     og[...] = jnp.concatenate([total / qgain[...], total / kgain[...]], axis=0)
 
-    z_fwd(1).wait_send()
     for h in range(2):
         x_fwd(h).wait_send()
         x_bwd(h).wait_send()
-        z_bwd(h).wait_send()
+        for hop in (z_first, z_second, back_first, back_second):
+            for n in range(2):
+                hop(h, n).wait_send()
         for n in range(3):
             stat_copy(h, n).wait_send()
     for step in STEPS:
@@ -548,15 +582,17 @@
         pltpu.VMEM((6, tile, HD), F32),
         pltpu.VMEM((2, HD, tile), BF16),
         pltpu.VMEM((2, HD, tile), BF16),
-        pltpu.VMEM((2, HD, tile), BF16),
-        pltpu.VMEM((2, HD, tile), BF16),
+        pltpu.VMEM((2, 2, HD // 2, tile), BF16),
+        pltpu.VMEM((2, 2, HD // 2, tile), BF16),
+        pairs(2),
+        pltpu.VMEM((2, 2, HD // 2, tile), BF16),
         pltpu.VMEM((3, 2, 2, tile, HD), F32),
         pairs(2, 2, 3), pairs(2, 2, 3), pairs(2, 2), pairs(2, 2),
         pltpu.VMEM((6, 8, HD), F32),
         pltpu.VMEM((3, most, 8, HD), F32),
-        dma((2,)), dma((2,)), dma((2,)), dma((2,)),
+        dma((2, 2)), dma((2, 2)), dma((2, 2)), dma((2, 2)), dma((2,)), dma((2,)),
         dma((2,)), dma((2,)), dma((2, 3)), dma((2, 3)),
-        dma((2,)), dma((2,)), dma((2,)), dma((2,)),
+        dma((2, 2)), dma((2, 2)), dma((2, 2)), dma((2, 2)), dma((2,)), dma((2,)),
         dma((2, 2)), dma((2, 2)), dma((2, 2)), dma((2, 2)),
         dma((2, 3)), dma((2, 3)),
         dma((3, most)), dma((3, most)),

time: 111 us -> 113 us (1.018)
    pallas_call x1, Pallas kernels: 108 us -> 110 us  [on_device(): pl.pallas_call(functools.partial(kernel, T, C, R, H, tile, chunk), out_sh...]
where the time goes in v3:
time: 113 us
  Pallas kernels  112 us (99%)
    pallas_call x1, Pallas kernels, on_device(): pl.pallas_call(functools.partial(kernel, T, C, R, H, tile, chunk), out_sh...  110 us
    pallas_call x1, Pallas kernels, on_device(): pl.pallas_call(hand_over, out_shape=(whole, whole, whole, jax.ShapeDtypeS...  2.47 us

profile of v3, /device:TPU:1, one launch (start us, length us, event | category | flops | bytes accessed | tf_op | source)
XLA Modules:
  0.0 112.9 jit_solution(2597848620855898182)
XLA Ops:
  0.6 109.7 %shard_map.111 = (bf16[6,256,128]{2,1,0:T(8,128)(2,1)}, bf16[6,256,128]{2,1,0:T(8,128)(2,1)}, bf16[6,256,128]{2,1,0:T(8,128)(2,1)}, f32[2,128]{1,0:T(2,128)}) custom-call(s32[3,6]{1,0:T(4,128)} %bitcast.14, s32[4,8,8]{2,1,0:T(8,128)} %counts.1, f32[1,128]{1,0:T(1,128)} %bitcast.16, f32[1,128]{1,0:T(1,128)} %bitcast.17, bf16[256,768]{1,0:T(8,128)(2,1)} %bitcast.10, ...), custom_call_target="tpu_custom_call" | custom-call | tf_op jit(solution)/shard_map/pallas_call | solution.py:602
  110.4 2.5 %shard_map.112 = (bf16[256,768]{1,0:T(8,128)(2,1)}, bf16[256,768]{1,0:T(8,128)(2,1)}, bf16[256,768]{1,0:T(8,128)(2,1)}, f32[2,128]{1,0:T(2,128)}) custom-call(s32[3,6]{1,0:T(4,128)} %bitcast.15, bf16[6,256,128]{2,1,0:T(8,128)(2,1)} %get-tuple-element.12.q, bf16[6,256,128]{2,1,0:T(8,128)(2,1)} %get-tuple-element.13.k, ...), custom_call_target="tpu_custom_call" | custom-call | tf_op jit(solution)/shard_map/pallas_call | solution.py:622

commit v4 on v2

v4 whole, which is shorter than its diff:
```python
import functools

import jax
import jax.numpy as jnp
from jax import lax
from jax.experimental import pallas as pl
from jax.experimental.pallas import tpu as pltpu
from jax.sharding import PartitionSpec as P

MESH = pl.DeviceIdType.MESH
HD = 128
F32 = jnp.float32
BF16 = jnp.bfloat16
SCALE = HD**-0.5
LOG2E = 1.4426950408889634
NT = (((1,), (1,)), ((), ()))
NN = (((1,), (0,)), ((), ()))
TN = (((0,), (0,)), ((), ()))

TIME, SPACE = 2, 4


def dot(a, b, dims):
    return lax.dot_general(a, b, dims, preferred_element_type=F32)


def unit_of(raw):
    x = raw.astype(F32)
    inv = lax.rsqrt(jnp.mean(x * x, axis=1, keepdims=True) + 1e-6)
    return x * inv, inv


def fold(x):
    return jnp.sum(x.reshape(x.shape[0] // 8, 8, x.shape[1]), axis=0)


def kernel(
    T, C, R, H, tile, chunk,
    we, counts, qgain, kgain, qraw, kraw, vals, ograd,
    oq, ok, ov, og,
    hq, hk, hv, ho, qd, kv, pp, dd, stats, sto, sti, dqt, fk, fv,
    xout, xin, zout, zin, rowo, rowi, colo, coli, gacc, gbuf,
    zf_s, zf_r, xf_s, xf_r, cf_s, cf_r, rf_s, rf_r,
    zb_s, zb_r, xb_s, xb_r, cb_s, cb_r, rb_s, rb_r, st_s, st_r, g_s, g_r,
):
    tm = lax.axis_index("tm")
    r = lax.axis_index("space")
    hd = lax.axis_index("head")
    t = lax.div(tm, C)
    c = lax.rem(tm, C)
    tz = t + 1 - 2 * lax.rem(t, 2)
    tx = lax.rem(t + 2, T)
    td = lax.rem(tz + 2, T)

    def dev(t_, c_, r_, h_):
        return (t_ * C + c_, r_, h_)

    def loop(n, body):
        def step(i, carry):
            body(i)
            return carry

        lax.fori_loop(0, n, step, 0)

    def on(condition, action):
        pl.when(condition)(action)

    G0 = T * H
    gi = t * H + hd

    def peer0(j):
        g = lax.rem(gi + j, G0)
        return dev(lax.div(g, H), c, r, lax.rem(g, H))

    def peer1(j):
        return dev(t, lax.rem(c + j, C), r, hd)

    def peer2(j):
        return dev(t, c, lax.rem(r + j, R), hd)

    groups = ((G0, gi, peer0), (C, c, peer1), (R, r, peer2))
    barrier = pltpu.get_barrier_semaphore()
    for size, _, peer in groups:

        def greet(j, peer=peer):
            pl.semaphore_signal(barrier, inc=1, device_id=peer(j + 1), device_id_type=MESH)

        loop(size - 1, greet)

    kinds = [we[0, h] + 2 * we[1, h] for h in range(6)]
    head_of = []
    for kind in range(3):
        low, high = jnp.int32(5), jnp.int32(0)
        for h in range(6):
            low = jnp.minimum(low, jnp.where(kinds[h] == kind, h, 5))
            high = jnp.maximum(high, jnp.where(kinds[h] == kind, h, 0))
        head_of += [low, high]

    def split(h):
        cut = pl.ds(pl.multiple_of(h * HD, HD), HD)
        for by_head, whole in ((hk, kraw), (hv, vals), (hq, qraw), (ho, ograd)):
            by_head[h] = whole[:, cut]

    loop(6, split)

    def raw(ref, slot):
        at = head_of[0]
        for s in range(1, 6):
            at = jnp.where(slot == s, head_of[s], at)
        return ref[at]

    def normed(x, gain):
        unit, _ = unit_of(x)
        return (unit * gain[...]).astype(BF16)

    def count_at(t_, c_, r_):
        inside = (c_ >= 0) & (c_ < C) & (r_ >= 0) & (r_ < R)
        got = counts[t_, lax.rem(c_ + C, C), lax.rem(r_ + R, R)]
        return jnp.where(inside, got, 0)

    own_count = count_at(t, c, r)
    lanes = lax.broadcasted_iota(jnp.int32, (1, tile), 1)
    query_ok = lanes < own_count
    rows_iota = lax.broadcasted_iota(jnp.int32, (chunk, tile), 0)

    def time_row(h, b):
        return 4 + 3 * h + b

    def kv_pair(p):
        return kv.at[pl.ds(4 + 2 * p, 2)]

    def side(step):
        return (step + 1) // 2

    def c_ok(step):
        return (c + step >= 0) & (c + step < C)

    def r_ok(step):
        return (r + step >= 0) & (r + step < R)

    def c_dev(step):
        return dev(t, lax.rem(c + step + C, C), r, hd)

    def r_dev(step):
        return dev(t, c, lax.rem(r + step + R, R), hd)

    def copy(src, dst, send, recv, where):
        return pltpu.make_async_remote_copy(
            src_ref=src, dst_ref=dst, send_sem=send, recv_sem=recv, device_id=where, device_id_type=MESH
        )

    def col_fwd(step):
        return copy(kv_pair(4), kv_pair(4 - step), cf_s.at[side(step)], cf_r.at[side(-step)], c_dev(step))

    def row_fwd(step, dc):
        return copy(
            kv_pair(4 + dc), kv_pair(4 + dc - 3 * step),
            rf_s.at[side(step), 1 + dc], rf_r.at[side(-step), 1 + dc], r_dev(step),
        )

    def z_fwd(h):
        return copy(qd.at[4 + 3 * h], qd.at[5 + 3 * h], zf_s.at[h], zf_r.at[h], dev(tz, c, r, hd))

    def x_fwd(h):
        return copy(qd.at[5 + 3 * h], qd.at[6 + 3 * h], xf_s.at[h], xf_r.at[h], dev(tx, c, r, hd))

    def x_bwd(h):
        return copy(xout.at[h], xin.at[h], xb_s.at[h], xb_r.at[h], dev(tx, c, r, hd))

    def z_bwd(h):
        return copy(zout.at[h], zin.at[h], zb_s.at[h], zb_r.at[h], dev(tz, c, r, hd))

    def row_bwd(step, h):
        return copy(
            rowo.at[h, side(step)], rowi.at[h, side(-step)],
            rb_s.at[h, side(step)], rb_r.at[h, side(-step)], r_dev(step),
        )

    def col_bwd(step, h):
        return copy(
            colo.at[h, side(step)], coli.at[h, side(-step)],
            cb_s.at[h, side(step)], cb_r.at[h, side(-step)], c_dev(step),
        )

    others = (tz, tx, td)

    def stat_copy(h, n):
        return copy(sto.at[h], sti.at[h, n], st_s.at[h, n], st_r.at[h, n], dev(others[n], c, r, hd))

    STEPS = (-1, 1)

    pl.semaphore_wait(barrier, G0 - 1 + C - 1 + R - 1)

    def norm_step(i):
        slot = jnp.where(i < 2, i + 4, jnp.where(i < 4, i, i - 4))
        row = jnp.where(i < 2, i + 2, jnp.where(i < 4, 3 * i - 2, i - 4))
        at = jnp.where(i < 2, i + 12, jnp.where(i < 4, i, i - 4))
        kv[at, 0] = normed(raw(hk, slot), kgain)
        kv[at, 1] = raw(hv, slot)
        qd[row, 0] = normed(raw(hq, slot), qgain)
        qd[row, 1] = raw(ho, slot)

        @pl.when(i == 1)
        def _():
            for step in STEPS:
                on(c_ok(step), col_fwd(step).start)
            for step in STEPS:
                on(r_ok(step), row_fwd(step, 0).start)

        on(i == 2, z_fwd(0).start)

    loop(6, norm_step)

    nothing = jnp.zeros((2, 2, tile, HD), BF16)
    for step in STEPS:

        def blank_column(i, step=step):
            kv[pl.ds(4 + 2 * (3 * i + 1 + step), 2)] = nothing

        def blank_row(i, step=step):
            kv[pl.ds(4 + 2 * (3 + 3 * step + i), 2)] = nothing

        on(jnp.logical_not(c_ok(step)), functools.partial(loop, 3, blank_column))
        on(jnp.logical_not(r_ok(step)), functools.partial(loop, 3, blank_row))

    def clear(i):
        stats[i] = jnp.zeros((16, tile), F32)
        dqt[i] = jnp.zeros((HD, tile), F32)
        fk[i] = jnp.zeros((tile, HD), F32)
        fv[i] = jnp.zeros((tile, HD), F32)

    loop(10, clear)
    gacc[...] = jnp.zeros_like(gacc)

    def pass_one(idx, row, at, count):
        query, up = qd[row, 0], qd[row, 1]
        sum_l, sum_d = stats[row, 0:8], stats[row, 8:16]
        for j in range(0, tile, chunk):
            s = dot(kv[at, 0, j : j + chunk], query, NT)
            p = jnp.where(rows_iota < count - j, jnp.exp2(s * (SCALE * LOG2E)), 0.0)
            dp = dot(kv[at, 1, j : j + chunk], up, NT)
            pp[idx, j : j + chunk] = p
            dd[idx, j : j + chunk] = dp
            sum_l = sum_l + fold(p)
            sum_d = sum_d + fold(p * dp)
        stats[row, 0:8] = sum_l
        stats[row, 8:16] = sum_d

    def pass_two(idx, row, at, slot, emit):
        query, up = qd[row, 0], qd[row, 1]
        inv, out_dot = stats[row, 0:1], stats[row, 8:9]
        key_sum = gacc[slot]
        dq = dqt[row]
        for j in range(0, tile, chunk):
            w = pp[idx, j : j + chunk] * inv
            g = (w * (dd[idx, j : j + chunk] - out_dot)).astype(BF16)
            keys = kv[at, 0, j : j + chunk]
            dk = dot(g, query, NN)
            dv = dot(w.astype(BF16), up, NN)
            dq = dq + dot(keys, g, TN)
            key_sum = key_sum + fold(dk * keys.astype(F32))
            emit(j, dk, dv)
        gacc[slot] = key_sum
        dqt[row] = dq

    def added_to(place):
        def emit(j, dk, dv):
            fk[place, pl.ds(j, chunk)] += dk
            fv[place, pl.ds(j, chunk)] += dv

        return emit

    def put_stats(row, total, dot_total, ok_lanes):
        inv = 1.0 / total
        stats[row, 0:8] = jnp.broadcast_to(jnp.where(ok_lanes, inv, 0.0), (8, tile))
        stats[row, 8:16] = jnp.broadcast_to(dot_total * inv, (8, tile))

    def partial(row):
        total = jnp.sum(stats[row, 0:8], axis=0, keepdims=True)
        return total, jnp.sum(stats[row, 8:16], axis=0, keepdims=True)

    def first(i):
        @pl.when(i == 3)
        def _():
            z_fwd(1).start()
            for dc in STEPS:
                on(c_ok(dc), col_fwd(-dc).wait_recv)
            for dc in STEPS:
                for step in STEPS:
                    on(c_ok(dc) & r_ok(step), row_fwd(step, dc).start)

        @pl.when(i == 5)
        def _():
            for dr in STEPS:
                on(r_ok(dr), row_fwd(-dr, 0).wait_recv)

        @pl.when(i == 7)
        def _():
            z_fwd(0).wait_recv()
            x_fwd(0).start()
            for dr in STEPS:
                for dc in STEPS:
                    on(r_ok(dr) & c_ok(dc), row_fwd(-dr, dc).wait_recv)

        p = jnp.int32(4)
        for n, q in ((3, 3), (4, 5), (5, 1), (6, 7), (7, 0), (8, 2), (9, 6), (10, 8)):
            p = jnp.where(i == n, q, p)
        dr = lax.div(p, 3)
        count = count_at(t, c + p - 3 * dr - 1, r + dr - 1)
        for h in range(2):
            row = jnp.where(i == 1, h, jnp.where(i == 2, 4 + 3 * h, 2 + h))
            at = jnp.where(i == 1, h, jnp.where(i == 2, 2 + h, 4 + 2 * p + h))
            idx = jnp.where(i == 1, h, jnp.where(i == 2, 4 + 3 * h, 10 + 2 * p + h))
            pass_one(idx, row, at, count)

    loop(11, first)

    far_count = jnp.where((td - t) * (td - t) == 1, own_count, 0)
    tile_ok = (query_ok, lanes < count_at(tz, c, r), lanes < count_at(td, c, r))

    def time_first(h):
        def step(i):
            on(i == 1, x_fwd(h).wait_recv)
            row = time_row(h, 1 + i)
            pass_one(row, row, 2 + h, jnp.where(i == 1, far_count, own_count))

        loop(2, step)
        for b in range(3):
            total, dot_total = partial(time_row(h, b))
            sto[h, 2 * b : 2 * b + 1] = total
            sto[h, 2 * b + 1 : 2 * b + 2] = dot_total
        sto[h, 6:8] = jnp.zeros((2, tile), F32)
        for n in range(3):
            stat_copy(h, n).start()

    def time_total(h):
        for n in range(3):
            stat_copy(h, n).wait_recv()
        for b, (n, i), (m, k) in ((0, (0, 2), (2, 4)), (1, (0, 0), (1, 4)), (2, (2, 0), (1, 2))):

            def row(q, b=b, n=n, i=i, m=m, k=k):
                mine = sto[h, 2 * b + q : 2 * b + q + 1]
                return mine + sti[h, n, i + q : i + q + 1] + sti[h, m, k + q : k + q + 1]

            put_stats(time_row(h, b), row(0), row(1), tile_ok[b])

    def time_second(h):
        time_total(h)

        def step(i):
            @pl.when(i == 1)
            def _():
                xout[h] = dqt[time_row(h, 2)].astype(BF16)
                x_bwd(h).start()

            row = time_row(h, 2 - i)
            pass_two(row, row, 2 + h, TIME + h, added_to(TIME + h))

        loop(3, step)

    def time_send_back(h):
        x_bwd(h).wait_recv()
        zout[h] = (dqt[time_row(h, 1)] + xin[h].astype(F32)).astype(BF16)
        z_bwd(h).start()

    time_first(0)
    loop(4, lambda row: put_stats(row, *partial(row), query_ok))

    def outer(i):
        d = lax.div(i, 3)
        dc = i - 3 * d

        @pl.when(i == 3)
        def _():
            for h in range(2):
                on(r_ok(-1), row_bwd(-1, h).start)

        for h in range(2):

            def emit(j, dk, dv, h=h):
                rowo[h, d, dc, 0, pl.ds(j, chunk)] = dk.astype(BF16)
                rowo[h, d, dc, 1, pl.ds(j, chunk)] = dv.astype(BF16)

            p = 6 * d + dc
            pass_two(10 + 2 * p + h, 2 + h, 4 + 2 * p + h, SPACE + h, emit)

    loop(6, outer)
    for h in range(2):
        on(r_ok(1), row_bwd(1, h).start)

    time_second(0)
    z_fwd(1).wait_recv()
    x_fwd(1).start()
    time_send_back(0)
    time_first(1)

    def middle(i):
        p = 2 + i
        for h in range(2):
            idx = jnp.where(i == 0, h, 10 + 2 * p + h)
            row = jnp.where(i == 0, h, 2 + h)
            at = jnp.where(i == 0, h, 4 + 2 * p + h)
            slot = jnp.where(i == 0, h, SPACE + h)
            place = jnp.where(i == 0, h, jnp.where(i == 1, 6 + h, jnp.where(i == 2, SPACE + h, 8 + h)))
            pass_two(idx, row, at, slot, added_to(place))

    loop(4, middle)

    for h in range(2):
        for dr in STEPS:

            def add_row(dr=dr, h=h):
                row_bwd(-dr, h).wait_recv()

                def add(i):
                    place = jnp.where(i == 1, SPACE + h, 6 + i + h)
                    fk[place] += rowi[h, side(dr), i, 0].astype(F32)
                    fv[place] += rowi[h, side(dr), i, 1].astype(F32)

                loop(3, add)

            on(r_ok(dr), add_row)
        for step in STEPS:

            def send_column(step=step, h=h):
                colo[h, side(step), 0] = fk[7 + step + h].astype(BF16)
                colo[h, side(step), 1] = fv[7 + step + h].astype(BF16)
                col_bwd(step, h).start()

            on(c_ok(step), send_column)

    time_second(1)
    time_send_back(1)

    pair_sum = gacc[0]
    for s in range(1, 6):
        pair_sum = pair_sum + gacc[s]

    def gain_copy(n, j):
        _, mine, peer = groups[n]
        return copy(gbuf.at[n, mine], gbuf.at[n, mine], g_s.at[n, j], g_r.at[n, mine], peer(j))

    def gain_send(n, value):
        size, mine, _ = groups[n]
        gbuf[n, mine] = value
        loop(size - 1, lambda j: gain_copy(n, j + 1).start())

    def gain_sum(n):
        size, mine, peer = groups[n]

        def wait(j):
            other = lax.rem(mine + j + 1, size)
            copy(gbuf.at[n, other], gbuf.at[n, other], g_s.at[n, j + 1], g_r.at[n, other], peer(j + 1)).wait_recv()

        loop(size - 1, wait)
        total = gbuf[n, 0]
        for i in range(1, size):
            total = total + gbuf[n, i]
        return total

    def query_out(s, grad_t):
        grad = jnp.transpose(grad_t) * SCALE
        unit, inv = unit_of(raw(hq, s))
        scaled = grad * qgain[...]
        mean = jnp.mean(scaled * unit, axis=1, keepdims=True)
        oq[s] = (inv * (scaled - unit * mean)).astype(BF16)

    def key_out(s):
        grad = fk[s] * SCALE
        unit, inv = unit_of(raw(hk, s))
        scaled = grad * kgain[...]
        mean = jnp.mean(scaled * unit, axis=1, keepdims=True)
        ok[s] = (inv * (scaled - unit * mean)).astype(BF16)
        ov[s] = fv[s].astype(BF16)

    gain_send(0, pair_sum)
    loop(4, lambda i: query_out(jnp.where(i < 2, i, i + 2), dqt[i]))
    gain_send(1, gain_sum(0))
    for h in range(2):
        for dc in STEPS:

            def add_column(dc=dc, h=h):
                col_bwd(-dc, h).wait_recv()
                fk[SPACE + h] += coli[h, side(dc), 0].astype(F32)
                fv[SPACE + h] += coli[h, side(dc), 1].astype(F32)

            on(c_ok(dc), add_column)
    loop(6, key_out)
    gain_send(2, gain_sum(1))
    for h in range(2):
        z_bwd(h).wait_recv()
    loop(2, lambda h: query_out(TIME + h, dqt[time_row(h, 0)] + zin[h].astype(F32)))
    total = jnp.sum(gain_sum(2), axis=0, keepdims=True) * SCALE
    og[...] = jnp.concatenate([total / qgain[...], total / kgain[...]], axis=0)

    for h in range(2):
        for made in (z_fwd, x_fwd, x_bwd, z_bwd):
            made(h).wait_send()
        for n in range(3):
            stat_copy(h, n).wait_send()
    for step in STEPS:
        on(c_ok(step), col_fwd(step).wait_send)
        on(r_ok(step), row_fwd(step, 0).wait_send)
        for dc in STEPS:
            on(c_ok(dc) & r_ok(step), row_fwd(step, dc).wait_send)
        for h in range(2):
            on(r_ok(step), row_bwd(step, h).wait_send)
            on(c_ok(step), col_bwd(step, h).wait_send)
    for n, (size, _, _) in enumerate(groups):
        loop(size - 1, lambda j, n=n: gain_copy(n, j + 1).wait_send())


def hand_over(we, q, k, v, gains, oq, ok, ov, og):
    kinds = [we[0, h] + 2 * we[1, h] for h in range(6)]
    for h in range(6):
        slot = 2 * kinds[h]
        for g in range(h):
            slot = slot + jnp.where(kinds[g] == kinds[h], 1, 0)
        for src, dst in ((q, oq), (k, ok), (v, ov)):
            dst[:, h * HD : (h + 1) * HD] = src[slot]
    og[...] = gains[...]


def on_device(T, C, R, H, query_raw, key_raw, values, out_grad, query_gain, key_gain, window_extent, tile_counts):
    tile, width = query_raw.shape[2], query_raw.shape[3]
    chunk = min(128, tile)
    flat = lambda x: x.reshape(tile, width)
    most = max(T * H, C, R)
    dma = pltpu.SemaphoreType.DMA
    vmem = pl.BlockSpec(memory_space=pltpu.VMEM)
    smem = pl.BlockSpec(memory_space=pltpu.SMEM)
    heads = lambda n: pltpu.VMEM((n, tile, HD), BF16)
    pairs = lambda *n: pltpu.VMEM(n + (2, tile, HD), BF16)
    scratch = [
        heads(6), heads(6), heads(6), heads(6),
        pairs(10), pairs(22),
        pltpu.VMEM((28, tile, tile), F32),
        pltpu.VMEM((28, tile, tile), F32),
        pltpu.VMEM((10, 16, tile), F32),
        pltpu.VMEM((2, 8, tile), F32),
        pltpu.VMEM((2, 3, 8, tile), F32),
        pltpu.VMEM((10, HD, tile), F32),
        pltpu.VMEM((10, tile, HD), F32),
        pltpu.VMEM((10, tile, HD), F32),
        pltpu.VMEM((2, HD, tile), BF16),
        pltpu.VMEM((2, HD, tile), BF16),
        pltpu.VMEM((2, HD, tile), BF16),
        pltpu.VMEM((2, HD, tile), BF16),
        pairs(2, 2, 3), pairs(2, 2, 3), pairs(2, 2), pairs(2, 2),
        pltpu.VMEM((6, 8, HD), F32),
        pltpu.VMEM((3, most, 8, HD), F32),
        dma((2,)), dma((2,)), dma((2,)), dma((2,)),
        dma((2,)), dma((2,)), dma((2, 3)), dma((2, 3)),
        dma((2,)), dma((2,)), dma((2,)), dma((2,)),
        dma((2, 2)), dma((2, 2)), dma((2, 2)), dma((2, 2)),
        dma((2, 3)), dma((2, 3)),
        dma((3, most)), dma((3, most)),
    ]
    wide = jax.ShapeDtypeStruct((6, tile, HD), BF16)
    extent = window_extent.T
    grad_q, grad_k, grad_v, gains = pl.pallas_call(
        functools.partial(kernel, T, C, R, H, tile, chunk),
        out_shape=(wide, wide, wide, jax.ShapeDtypeStruct((2, HD), F32)),
        in_specs=[smem, smem] + [vmem] * 6,
        out_specs=(vmem,) * 4,
        scratch_shapes=scratch,
        compiler_params=pltpu.CompilerParams(
            collective_id=0, has_side_effects=True, vmem_limit_bytes=60 * 1024 * 1024
        ),
    )(
        extent,
        tile_counts,
        query_gain.reshape(1, HD),
        key_gain.reshape(1, HD),
        flat(query_raw),
        flat(key_raw),
        flat(values),
        flat(out_grad),
    )
    whole = jax.ShapeDtypeStruct((tile, width), BF16)
    outs = pl.pallas_call(
        hand_over,
        out_shape=(whole, whole, whole, jax.ShapeDtypeStruct((2, HD), F32)),
        in_specs=[smem] + [vmem] * 4,
        out_specs=(vmem,) * 4,
        compiler_params=pltpu.CompilerParams(vmem_limit_bytes=60 * 1024 * 1024),
    )(extent, grad_q, grad_k, grad_v, gains)
    shape = (1, 1, tile, width)
    return tuple(x.reshape(shape) for x in outs[:3]) + (outs[3],)


def solution(mesh):
    tile_spec = P("tm", "space", None, "head")

    def program(*args):
        T = args[7].shape[0]
        C = mesh.shape["tm"] // T
        return on_device(T, C, mesh.shape["space"], mesh.shape["head"], *args)

    return jax.shard_map(
        program,
        mesh=mesh,
        in_specs=(tile_spec,) * 4 + (P(), P(), P("head", None), P()),
        out_specs=(tile_spec,) * 3 + (P(),),
        check_vma=False,
    )
```

time: 111 us -> 106 us (0.955)
  Pallas kernels: 111 us -> 105 us
    pallas_call x1, Pallas kernels: 108 us -> 102 us  [on_device(): pl.pallas_call(functools.partial(kernel, T, C, R, H, tile, chunk), out_sh...]
where the time goes in v4:
time: 106 us
  Pallas kernels  105 us (99%)
    pallas_call x1, Pallas kernels, on_device(): pl.pallas_call(functools.partial(kernel, T, C, R, H, tile, chunk), out_sh...  102 us
    pallas_call x1, Pallas kernels, on_device(): pl.pallas_call(hand_over, out_shape=(whole, whole, whole, jax.ShapeDtypeS...  2.47 us

profile of v4, /device:TPU:1, one launch (start us, length us, event | category | flops | bytes accessed | tf_op | source)
XLA Modules:
  0.0 105.6 jit_solution(13092704524833365871)
XLA Ops:
  0.6 102.5 %shard_map.111 = (bf16[6,256,128]{2,1,0:T(8,128)(2,1)}, bf16[6,256,128]{2,1,0:T(8,128)(2,1)}, bf16[6,256,128]{2,1,0:T(8,128)(2,1)}, f32[2,128]{1,0:T(2,128)}) custom-call(s32[3,6]{1,0:T(4,128)} %bitcast.14, s32[4,8,8]{2,1,0:T(8,128)} %counts.1, f32[1,128]{1,0:T(1,128)} %bitcast.16, f32[1,128]{1,0:T(1,128)} %bitcast.17, bf16[256,768]{1,0:T(8,128)(2,1)} %bitcast.10, ...), custom_call_target="tpu_custom_call" | custom-call | tf_op jit(solution)/shard_map/pallas_call | solution.py:561
  103.1 2.5 %shard_map.112 = (bf16[256,768]{1,0:T(8,128)(2,1)}, bf16[256,768]{1,0:T(8,128)(2,1)}, bf16[256,768]{1,0:T(8,128)(2,1)}, f32[2,128]{1,0:T(2,128)}) custom-call(s32[3,6]{1,0:T(4,128)} %bitcast.15, bf16[6,256,128]{2,1,0:T(8,128)(2,1)} %get-tuple-element.12.q, bf16[6,256,128]{2,1,0:T(8,128)(2,1)} %get-tuple-element.13.k, ...), custom_call_target="tpu_custom_call" | custom-call | tf_op jit(solution)/shard_map/pallas_call | solution.py:581

commit v5 on v4

--- a/solution.py
+++ b/solution.py
@@ -126,8 +126,8 @@
     def time_row(h, b):
         return 4 + 3 * h + b
 
-    def kv_pair(p):
-        return kv.at[pl.ds(4 + 2 * p, 2)]
+    def tile_of(p, h):
+        return kv.at[4 + 2 * p + h]
 
     def side(step):
         return (step + 1) // 2
@@ -149,13 +149,15 @@
             src_ref=src, dst_ref=dst, send_sem=send, recv_sem=recv, device_id=where, device_id_type=MESH
         )
 
-    def col_fwd(step):
-        return copy(kv_pair(4), kv_pair(4 - step), cf_s.at[side(step)], cf_r.at[side(-step)], c_dev(step))
-
-    def row_fwd(step, dc):
+    def col_fwd(step, h):
         return copy(
-            kv_pair(4 + dc), kv_pair(4 + dc - 3 * step),
-            rf_s.at[side(step), 1 + dc], rf_r.at[side(-step), 1 + dc], r_dev(step),
+            tile_of(4, h), tile_of(4 - step, h), cf_s.at[h, side(step)], cf_r.at[h, side(-step)], c_dev(step)
+        )
+
+    def row_fwd(step, dc, h):
+        return copy(
+            tile_of(4 + dc, h), tile_of(4 + dc - 3 * step, h),
+            rf_s.at[h, side(step), 1 + dc], rf_r.at[h, side(-step), 1 + dc], r_dev(step),
         )
 
     def z_fwd(h):
@@ -170,10 +172,10 @@
     def z_bwd(h):
         return copy(zout.at[h], zin.at[h], zb_s.at[h], zb_r.at[h], dev(tz, c, r, hd))
 
-    def row_bwd(step, h):
+    def row_bwd(step, h, i):
         return copy(
-            rowo.at[h, side(step)], rowi.at[h, side(-step)],
-            rb_s.at[h, side(step)], rb_r.at[h, side(-step)], r_dev(step),
+            rowo.at[h, side(step), i], rowi.at[h, side(-step), i],
+            rb_s.at[h, side(step), i], rb_r.at[h, side(-step), i], r_dev(step),
         )
 
     def col_bwd(step, h):
@@ -200,14 +202,12 @@
         qd[row, 0] = normed(raw(hq, slot), qgain)
         qd[row, 1] = raw(ho, slot)
 
-        @pl.when(i == 1)
+        @pl.when(i < 2)
         def _():
             for step in STEPS:
-                on(c_ok(step), col_fwd(step).start)
+                on(c_ok(step), col_fwd(step, i).start)
             for step in STEPS:
-                on(r_ok(step), row_fwd(step, 0).start)
-
-        on(i == 2, z_fwd(0).start)
+                on(r_ok(step), row_fwd(step, 0, i).start)
 
     loop(6, norm_step)
 
@@ -279,41 +279,43 @@
         total = jnp.sum(stats[row, 0:8], axis=0, keepdims=True)
         return total, jnp.sum(stats[row, 8:16], axis=0, keepdims=True)
 
-    def first(i):
-        @pl.when(i == 3)
-        def _():
-            z_fwd(1).start()
-            for dc in STEPS:
-                on(c_ok(dc), col_fwd(-dc).wait_recv)
-            for dc in STEPS:
-                for step in STEPS:
-                    on(c_ok(dc) & r_ok(step), row_fwd(step, dc).start)
-
-        @pl.when(i == 5)
-        def _():
-            for dr in STEPS:
-                on(r_ok(dr), row_fwd(-dr, 0).wait_recv)
-
-        @pl.when(i == 7)
-        def _():
-            z_fwd(0).wait_recv()
-            x_fwd(0).start()
-            for dr in STEPS:
-                for dc in STEPS:
-                    on(r_ok(dr) & c_ok(dc), row_fwd(-dr, dc).wait_recv)
-
-        p = jnp.int32(4)
-        for n, q in ((3, 3), (4, 5), (5, 1), (6, 7), (7, 0), (8, 2), (9, 6), (10, 8)):
-            p = jnp.where(i == n, q, p)
-        dr = lax.div(p, 3)
-        count = count_at(t, c + p - 3 * dr - 1, r + dr - 1)
+    def own(i):
         for h in range(2):
             row = jnp.where(i == 1, h, jnp.where(i == 2, 4 + 3 * h, 2 + h))
-            at = jnp.where(i == 1, h, jnp.where(i == 2, 2 + h, 4 + 2 * p + h))
-            idx = jnp.where(i == 1, h, jnp.where(i == 2, 4 + 3 * h, 10 + 2 * p + h))
-            pass_one(idx, row, at, count)
-
-    loop(11, first)
+            at = jnp.where(i == 1, h, jnp.where(i == 2, 2 + h, 12 + h))
+            idx = jnp.where(i == 1, h, jnp.where(i == 2, 4 + 3 * h, 18 + h))
+            pass_one(idx, row, at, own_count)
+
+    loop(3, own)
+
+    def space_count(p):
+        dr = lax.div(p, 3)
+        return count_at(t, c + p - 3 * dr - 1, r + dr - 1)
+
+    def cross(i):
+        @pl.when(i == 0)
+        def _():
+            for h in range(2):
+                for dc in STEPS:
+                    on(c_ok(dc), col_fwd(-dc, h).wait_recv)
+                for dc in STEPS:
+                    for step in STEPS:
+                        on(c_ok(dc) & r_ok(step), row_fwd(step, dc, h).start)
+            for h in range(2):
+                z_fwd(h).start()
+
+        @pl.when(i == 2)
+        def _():
+            for h in range(2):
+                for dr in STEPS:
+                    on(r_ok(dr), row_fwd(-dr, 0, h).wait_recv)
+
+        p = jnp.where(i < 2, 3 + 2 * i, 6 * i - 11)
+        count = space_count(p)
+        for h in range(2):
+            pass_one(10 + 2 * p + h, 2 + h, 4 + 2 * p + h, count)
+
+    loop(4, cross)
 
     far_count = jnp.where((td - t) * (td - t) == 1, own_count, 0)
     tile_ok = (query_ok, lanes < count_at(tz, c, r), lanes < count_at(td, c, r))
@@ -363,36 +365,41 @@
         zout[h] = (dqt[time_row(h, 1)] + xin[h].astype(F32)).astype(BF16)
         z_bwd(h).start()
 
-    time_first(0)
-    loop(4, lambda row: put_stats(row, *partial(row), query_ok))
-
-    def outer(i):
-        d = lax.div(i, 3)
-        dc = i - 3 * d
-
-        @pl.when(i == 3)
+    def corners(h):
+        @pl.when(h == 1)
         def _():
-            for h in range(2):
-                on(r_ok(-1), row_bwd(-1, h).start)
-
-        for h in range(2):
-
-            def emit(j, dk, dv, h=h):
-                rowo[h, d, dc, 0, pl.ds(j, chunk)] = dk.astype(BF16)
-                rowo[h, d, dc, 1, pl.ds(j, chunk)] = dv.astype(BF16)
-
-            p = 6 * d + dc
-            pass_two(10 + 2 * p + h, 2 + h, 4 + 2 * p + h, SPACE + h, emit)
-
-    loop(6, outer)
-    for h in range(2):
-        on(r_ok(1), row_bwd(1, h).start)
-
-    time_second(0)
-    z_fwd(1).wait_recv()
-    x_fwd(1).start()
-    time_send_back(0)
-    time_first(1)
+            z_fwd(0).wait_recv()
+            x_fwd(0).start()
+
+        for dr in STEPS:
+            for dc in STEPS:
+                on(r_ok(dr) & c_ok(dc), row_fwd(-dr, dc, h).wait_recv)
+
+        def corner(i):
+            for dc in range(0, 3, 2):
+                p = 6 * i + dc
+                pass_one(10 + 2 * p + h, 2 + h, 4 + 2 * p + h, space_count(p))
+
+        loop(2, corner)
+        put_stats(2 + h, *partial(2 + h), query_ok)
+
+        def outer(i):
+            dc = jnp.where(i == 0, 0, 3 - i)
+            for d in range(2):
+
+                def emit(j, dk, dv, d=d):
+                    rowo[h, d, dc, 0, pl.ds(j, chunk)] = dk.astype(BF16)
+                    rowo[h, d, dc, 1, pl.ds(j, chunk)] = dv.astype(BF16)
+
+                p = 6 * d + dc
+                pass_two(10 + 2 * p + h, 2 + h, 4 + 2 * p + h, SPACE + h, emit)
+            for step in STEPS:
+                on(r_ok(step), row_bwd(step, h, dc).start)
+
+        loop(3, outer)
+
+    loop(2, corners)
+    loop(2, lambda row: put_stats(row, *partial(row), query_ok))
 
     def middle(i):
         p = 2 + i
@@ -406,29 +413,34 @@
 
     loop(4, middle)
 
-    for h in range(2):
-        for dr in STEPS:
-
-            def add_row(dr=dr, h=h):
-                row_bwd(-dr, h).wait_recv()
-
-                def add(i):
-                    place = jnp.where(i == 1, SPACE + h, 6 + i + h)
+    def rows_back(h):
+        for i in (0, 2, 1):
+            place = SPACE + h if i == 1 else 6 + i + h
+            for dr in STEPS:
+
+                def add_row(dr=dr, i=i, place=place):
+                    row_bwd(-dr, h, i).wait_recv()
                     fk[place] += rowi[h, side(dr), i, 0].astype(F32)
                     fv[place] += rowi[h, side(dr), i, 1].astype(F32)
 
-                loop(3, add)
-
-            on(r_ok(dr), add_row)
-        for step in STEPS:
-
-            def send_column(step=step, h=h):
-                colo[h, side(step), 0] = fk[7 + step + h].astype(BF16)
-                colo[h, side(step), 1] = fv[7 + step + h].astype(BF16)
-                col_bwd(step, h).start()
-
-            on(c_ok(step), send_column)
-
+                on(r_ok(dr), add_row)
+            if i != 1:
+
+                def send_column(step=i - 1, place=place):
+                    colo[h, side(step), 0] = fk[place].astype(BF16)
+                    colo[h, side(step), 1] = fv[place].astype(BF16)
+                    col_bwd(step, h).start()
+
+                on(c_ok(i - 1), send_column)
+
+    z_fwd(1).wait_recv()
+    x_fwd(1).start()
+    time_first(0)
+    rows_back(0)
+    time_second(0)
+    time_first(1)
+    time_send_back(0)
+    rows_back(1)
     time_second(1)
     time_send_back(1)
 
@@ -476,6 +488,7 @@
     gain_send(0, pair_sum)
     loop(4, lambda i: query_out(jnp.where(i < 2, i, i + 2), dqt[i]))
     gain_send(1, gain_sum(0))
+    loop(4, key_out)
     for h in range(2):
         for dc in STEPS:
 
@@ -485,8 +498,8 @@
                 fv[SPACE + h] += coli[h, side(dc), 1].astype(F32)
 
             on(c_ok(dc), add_column)
-    loop(6, key_out)
     gain_send(2, gain_sum(1))
+    loop(2, lambda h: key_out(SPACE + h))
     for h in range(2):
         z_bwd(h).wait_recv()
     loop(2, lambda h: query_out(TIME + h, dqt[time_row(h, 0)] + zin[h].astype(F32)))
@@ -499,12 +512,13 @@
         for n in range(3):
             stat_copy(h, n).wait_send()
     for step in STEPS:
-        on(c_ok(step), col_fwd(step).wait_send)
-        on(r_ok(step), row_fwd(step, 0).wait_send)
-        for dc in STEPS:
-            on(c_ok(dc) & r_ok(step), row_fwd(step, dc).wait_send)
         for h in range(2):
-            on(r_ok(step), row_bwd(step, h).wait_send)
+            on(c_ok(step), col_fwd(step, h).wait_send)
+            on(r_ok(step), row_fwd(step, 0, h).wait_send)
+            for dc in STEPS:
+                on(c_ok(dc) & r_ok(step), row_fwd(step, dc, h).wait_send)
+            for i in range(3):
+                on(r_ok(step), row_bwd(step, h, i).wait_send)
             on(c_ok(step), col_bwd(step, h).wait_send)
     for n, (size, _, _) in enumerate(groups):
         loop(size - 1, lambda j, n=n: gain_copy(n, j + 1).wait_send())
@@ -550,9 +564,9 @@
         pltpu.VMEM((6, 8, HD), F32),
         pltpu.VMEM((3, most, 8, HD), F32),
         dma((2,)), dma((2,)), dma((2,)), dma((2,)),
-        dma((2,)), dma((2,)), dma((2, 3)), dma((2, 3)),
+        dma((2, 2)), dma((2, 2)), dma((2, 2, 3)), dma((2, 2, 3)),
         dma((2,)), dma((2,)), dma((2,)), dma((2,)),
-        dma((2, 2)), dma((2, 2)), dma((2, 2)), dma((2, 2)),
+        dma((2, 2)), dma((2, 2)), dma((2, 2, 3)), dma((2, 2, 3)),
         dma((2, 3)), dma((2, 3)),
         dma((3, most)), dma((3, most)),
     ]

time: 106 us -> 101 us (0.953)
  Pallas kernels: 105 us -> 99.8 us
    pallas_call x1, Pallas kernels: 102 us -> 97.3 us  [on_device(): pl.pallas_call(functools.partial(kernel, T, C, R, H, tile, chunk), out_sh...]
where the time goes in v5:
time: 101 us; the launch traced here: 100 us
  Pallas kernels  99.8 us (99%)
    pallas_call x1, Pallas kernels, on_device(): pl.pallas_call(functools.partial(kernel, T, C, R, H, tile, chunk), out_sh...  97.3 us
    pallas_call x1, Pallas kernels, on_device(): pl.pallas_call(hand_over, out_shape=(whole, whole, whole, jax.ShapeDtypeS...  2.47 us

profile of v5, /device:TPU:1, one launch (start us, length us, event | category | flops | bytes accessed | tf_op | source)
XLA Modules:
  0.0 100.4 jit_solution(370491831058772165)
XLA Ops:
  0.6 97.3 %shard_map.111 = (bf16[6,256,128]{2,1,0:T(8,128)(2,1)}, bf16[6,256,128]{2,1,0:T(8,128)(2,1)}, bf16[6,256,128]{2,1,0:T(8,128)(2,1)}, f32[2,128]{1,0:T(2,128)}) custom-call(s32[3,6]{1,0:T(4,128)} %bitcast.14, s32[4,8,8]{2,1,0:T(8,128)} %counts.1, f32[1,128]{1,0:T(1,128)} %bitcast.16, f32[1,128]{1,0:T(1,128)} %bitcast.17, bf16[256,768]{1,0:T(8,128)(2,1)} %bitcast.10, ...), custom_call_target="tpu_custom_call" | custom-call | tf_op jit(solution)/shard_map/pallas_call | solution.py:575
  97.9 2.5 %shard_map.112 = (bf16[256,768]{1,0:T(8,128)(2,1)}, bf16[256,768]{1,0:T(8,128)(2,1)}, bf16[256,768]{1,0:T(8,128)(2,1)}, f32[2,128]{1,0:T(2,128)}) custom-call(s32[3,6]{1,0:T(4,128)} %bitcast.15, bf16[6,256,128]{2,1,0:T(8,128)(2,1)} %get-tuple-element.12.q, bf16[6,256,128]{2,1,0:T(8,128)(2,1)} %get-tuple-element.13.k, ...), custom_call_target="tpu_custom_call" | custom-call | tf_op jit(solution)/shard_map/pallas_call | solution.py:595

commit v6 on v5

--- a/solution.py
+++ b/solution.py
@@ -280,6 +280,7 @@
         return total, jnp.sum(stats[row, 8:16], axis=0, keepdims=True)
 
     def own(i):
+        on(i == 2, z_fwd(0).start)
         for h in range(2):
             row = jnp.where(i == 1, h, jnp.where(i == 2, 4 + 3 * h, 2 + h))
             at = jnp.where(i == 1, h, jnp.where(i == 2, 2 + h, 12 + h))
@@ -301,8 +302,7 @@
                 for dc in STEPS:
                     for step in STEPS:
                         on(c_ok(dc) & r_ok(step), row_fwd(step, dc, h).start)
-            for h in range(2):
-                z_fwd(h).start()
+            z_fwd(1).start()
 
         @pl.when(i == 2)
         def _():
@@ -366,11 +366,6 @@
         z_bwd(h).start()
 
     def corners(h):
-        @pl.when(h == 1)
-        def _():
-            z_fwd(0).wait_recv()
-            x_fwd(0).start()
-
         for dr in STEPS:
             for dc in STEPS:
                 on(r_ok(dr) & c_ok(dc), row_fwd(-dr, dc, h).wait_recv)
@@ -383,6 +378,11 @@
         loop(2, corner)
         put_stats(2 + h, *partial(2 + h), query_ok)
 
+        @pl.when(h == 0)
+        def _():
+            z_fwd(0).wait_recv()
+            x_fwd(0).start()
+
         def outer(i):
             dc = jnp.where(i == 0, 0, 3 - i)
             for d in range(2):
@@ -398,7 +398,14 @@
 
         loop(3, outer)
 
+        @pl.when(h == 0)
+        def _():
+            time_first(0)
+
     loop(2, corners)
+    time_second(0)
+    z_fwd(1).wait_recv()
+    x_fwd(1).start()
     loop(2, lambda row: put_stats(row, *partial(row), query_ok))
 
     def middle(i):
@@ -433,15 +440,11 @@
 
                 on(c_ok(i - 1), send_column)
 
-    z_fwd(1).wait_recv()
-    x_fwd(1).start()
-    time_first(0)
+    time_send_back(0)
+    time_first(1)
     rows_back(0)
-    time_second(0)
-    time_first(1)
-    time_send_back(0)
+    time_second(1)
     rows_back(1)
-    time_second(1)
     time_send_back(1)
 
     pair_sum = gacc[0]
@@ -537,7 +540,7 @@
 
 def on_device(T, C, R, H, query_raw, key_raw, values, out_grad, query_gain, key_gain, window_extent, tile_counts):
     tile, width = query_raw.shape[2], query_raw.shape[3]
-    chunk = min(128, tile)
+    chunk = min(256, tile)
     flat = lambda x: x.reshape(tile, width)
     most = max(T * H, C, R)
     dma = pltpu.SemaphoreType.DMA

time: 101 us -> 106 us (1.050)
  Pallas kernels: 99.8 us -> 105 us
    pallas_call x1, Pallas kernels: 97.3 us -> 103 us  [on_device(): pl.pallas_call(functools.partial(kernel, T, C, R, H, tile, chunk), out_sh...]
where the time goes in v6:
time: 106 us
  Pallas kernels  105 us (99%)
    pallas_call x1, Pallas kernels, on_device(): pl.pallas_call(functools.partial(kernel, T, C, R, H, tile, chunk), out_sh...  103 us
    pallas_call x1, Pallas kernels, on_device(): pl.pallas_call(hand_over, out_shape=(whole, whole, whole, jax.ShapeDtypeS...  2.47 us

profile of v6, /device:TPU:1, one launch (start us, length us, event | category | flops | bytes accessed | tf_op | source)
XLA Modules:
  0.0 105.7 jit_solution(3483768444368693531)
XLA Ops:
  0.6 102.6 %shard_map.111 = (bf16[6,256,128]{2,1,0:T(8,128)(2,1)}, bf16[6,256,128]{2,1,0:T(8,128)(2,1)}, bf16[6,256,128]{2,1,0:T(8,128)(2,1)}, f32[2,128]{1,0:T(2,128)}) custom-call(s32[3,6]{1,0:T(4,128)} %bitcast.14, s32[4,8,8]{2,1,0:T(8,128)} %counts.1, f32[1,128]{1,0:T(1,128)} %bitcast.16, f32[1,128]{1,0:T(1,128)} %bitcast.17, bf16[256,768]{1,0:T(8,128)(2,1)} %bitcast.10, ...), custom_call_target="tpu_custom_call" | custom-call | tf_op jit(solution)/shard_map/pallas_call | solution.py:578
  103.2 2.5 %shard_map.112 = (bf16[256,768]{1,0:T(8,128)(2,1)}, bf16[256,768]{1,0:T(8,128)(2,1)}, bf16[256,768]{1,0:T(8,128)(2,1)}, f32[2,128]{1,0:T(2,128)}) custom-call(s32[3,6]{1,0:T(4,128)} %bitcast.15, bf16[6,256,128]{2,1,0:T(8,128)(2,1)} %get-tuple-element.12.q, bf16[6,256,128]{2,1,0:T(8,128)(2,1)} %get-tuple-element.13.k, ...), custom_call_target="tpu_custom_call" | custom-call | tf_op jit(solution)/shard_map/pallas_call | solution.py:598

commit v7 on v5

--- a/solution.py
+++ b/solution.py
@@ -301,11 +301,11 @@
                 for dc in STEPS:
                     for step in STEPS:
                         on(c_ok(dc) & r_ok(step), row_fwd(step, dc, h).start)
-            for h in range(2):
-                z_fwd(h).start()
+            z_fwd(0).start()
 
         @pl.when(i == 2)
         def _():
+            z_fwd(1).start()
             for h in range(2):
                 for dr in STEPS:
                     on(r_ok(dr), row_fwd(-dr, 0, h).wait_recv)
@@ -366,11 +366,6 @@
         z_bwd(h).start()
 
     def corners(h):
-        @pl.when(h == 1)
-        def _():
-            z_fwd(0).wait_recv()
-            x_fwd(0).start()
-
         for dr in STEPS:
             for dc in STEPS:
                 on(r_ok(dr) & c_ok(dc), row_fwd(-dr, dc, h).wait_recv)
@@ -399,6 +394,8 @@
         loop(3, outer)
 
     loop(2, corners)
+    z_fwd(0).wait_recv()
+    x_fwd(0).start()
     loop(2, lambda row: put_stats(row, *partial(row), query_ok))
 
     def middle(i):
@@ -437,10 +434,10 @@
     x_fwd(1).start()
     time_first(0)
     rows_back(0)
+    time_first(1)
     time_second(0)
-    time_first(1)
+    rows_back(1)
     time_send_back(0)
-    rows_back(1)
     time_second(1)
     time_send_back(1)
 

time: 101 us -> 99 us (0.980)
  Pallas kernels: 99.8 us -> 98.2 us
    pallas_call x1, Pallas kernels: 97.3 us -> 95.8 us  [on_device(): pl.pallas_call(functools.partial(kernel, T, C, R, H, tile, chunk), out_sh...]
where the time goes in v7:
time: 99 us; the launch traced here: 98.9 us
  Pallas kernels  98.2 us (99%)
    pallas_call x1, Pallas kernels, on_device(): pl.pallas_call(functools.partial(kernel, T, C, R, H, tile, chunk), out_sh...  95.8 us
    pallas_call x1, Pallas kernels, on_device(): pl.pallas_call(hand_over, out_shape=(whole, whole, whole, jax.ShapeDtypeS...  2.47 us

profile of v7, /device:TPU:1, one launch (start us, length us, event | category | flops | bytes accessed | tf_op | source)
XLA Modules:
  0.0 98.9 jit_solution(8012677568482006588)
XLA Ops:
  0.6 95.8 %shard_map.111 = (bf16[6,256,128]{2,1,0:T(8,128)(2,1)}, bf16[6,256,128]{2,1,0:T(8,128)(2,1)}, bf16[6,256,128]{2,1,0:T(8,128)(2,1)}, f32[2,128]{1,0:T(2,128)}) custom-call(s32[3,6]{1,0:T(4,128)} %bitcast.14, s32[4,8,8]{2,1,0:T(8,128)} %counts.1, f32[1,128]{1,0:T(1,128)} %bitcast.16, f32[1,128]{1,0:T(1,128)} %bitcast.17, bf16[256,768]{1,0:T(8,128)(2,1)} %bitcast.10, ...), custom_call_target="tpu_custom_call" | custom-call | tf_op jit(solution)/shard_map/pallas_call | solution.py:572
  96.4 2.5 %shard_map.112 = (bf16[256,768]{1,0:T(8,128)(2,1)}, bf16[256,768]{1,0:T(8,128)(2,1)}, bf16[256,768]{1,0:T(8,128)(2,1)}, f32[2,128]{1,0:T(2,128)}) custom-call(s32[3,6]{1,0:T(4,128)} %bitcast.15, bf16[6,256,128]{2,1,0:T(8,128)(2,1)} %get-tuple-element.12.q, bf16[6,256,128]{2,1,0:T(8,128)(2,1)} %get-tuple-element.13.k, ...), custom_call_target="tpu_custom_call" | custom-call | tf_op jit(solution)/shard_map/pallas_call | solution.py:592

commit v8 on v7

--- a/solution.py
+++ b/solution.py
@@ -534,7 +534,7 @@
 
 def on_device(T, C, R, H, query_raw, key_raw, values, out_grad, query_gain, key_gain, window_extent, tile_counts):
     tile, width = query_raw.shape[2], query_raw.shape[3]
-    chunk = min(128, tile)
+    chunk = min(256, tile)
     flat = lambda x: x.reshape(tile, width)
     most = max(T * H, C, R)
     dma = pltpu.SemaphoreType.DMA

time: 99 us -> 99 us (level)
  no operation moved by 1% of the time
where the time goes in v8:
time: 99 us; the launch traced here: 98.8 us
  Pallas kernels  98.1 us (99%)
    pallas_call x1, Pallas kernels, on_device(): pl.pallas_call(functools.partial(kernel, T, C, R, H, tile, chunk), out_sh...  95.7 us
    pallas_call x1, Pallas kernels, on_device(): pl.pallas_call(hand_over, out_shape=(whole, whole, whole, jax.ShapeDtypeS...  2.47 us

profile of v8, /device:TPU:1, one launch (start us, length us, event | category | flops | bytes accessed | tf_op | source)
XLA Modules:
  0.0 98.8 jit_solution(11145861508922860282)
XLA Ops:
  0.6 95.7 %shard_map.111 = (bf16[6,256,128]{2,1,0:T(8,128)(2,1)}, bf16[6,256,128]{2,1,0:T(8,128)(2,1)}, bf16[6,256,128]{2,1,0:T(8,128)(2,1)}, f32[2,128]{1,0:T(2,128)}) custom-call(s32[3,6]{1,0:T(4,128)} %bitcast.14, s32[4,8,8]{2,1,0:T(8,128)} %counts.1, f32[1,128]{1,0:T(1,128)} %bitcast.16, f32[1,128]{1,0:T(1,128)} %bitcast.17, bf16[256,768]{1,0:T(8,128)(2,1)} %bitcast.10, ...), custom_call_target="tpu_custom_call" | custom-call | tf_op jit(solution)/shard_map/pallas_call | solution.py:572
  96.3 2.5 %shard_map.112 = (bf16[256,768]{1,0:T(8,128)(2,1)}, bf16[256,768]{1,0:T(8,128)(2,1)}, bf16[256,768]{1,0:T(8,128)(2,1)}, f32[2,128]{1,0:T(2,128)}) custom-call(s32[3,6]{1,0:T(4,128)} %bitcast.15, bf16[6,256,128]{2,1,0:T(8,128)(2,1)} %get-tuple-element.12.q, bf16[6,256,128]{2,1,0:T(8,128)(2,1)} %get-tuple-element.13.k, ...), custom_call_target="tpu_custom_call" | custom-call | tf_op jit(solution)/shard_map/pallas_call | solution.py:592
